TPU v7x, 128 devices: a whole 4x4x4 slice. The times are simulated.
128 devices in a mesh: seqo: 4 (over z), seqi: 16 (over y, x_hi, core), chan: 2 (over x_lo).
Axes of the slice: x: 4 (x_hi: 2, x_lo: 2; x = x_hi * 2 + x_lo), y: 4, z: 4, core: 2. Of those that a mesh axis runs over, the one named last changes fastest.
Arguments:
- signal: float32 [48, 524288], P('chan', ('seqo', 'seqi')), may hold values from -6 to 6
- cotangent: float32 [48, 524288], P('chan', ('seqo', 'seqi')), may hold values from -0.0078125 to 0.0078125
- long_filter: float32 [48, 524288], P('chan', ('seqo', 'seqi')), may hold values from -6 to 6
Outputs:
- grad_signal: float32 [48, 524288], P('chan', ('seqo', 'seqi'))
- grad_filter: float32 [48, 524288], P('chan', ('seqo', 'seqi'))
All inputs are finite; a program needn't handle non-finite values.
Results may differ from a plain program's by a relative error of at most 0.000098.
Values sent between devices are 32-bit elements; how exact they have to be, the bound alone decides.
No kernel may reach another device: no remote copies, remote signals or barrier semaphores. Data moves between devices by JAX's collectives and lax.ppermute only.
A program may use at most 128 MiB of HBM per device.

v0:
```python
import functools
import math

import jax
import jax.numpy as jnp
import ml_dtypes
import numpy as np
from jax import lax
from jax.experimental import pallas as pl
from jax.experimental.pallas import tpu as pltpu
from jax.sharding import PartitionSpec as P

LANES = 128
OUTER = 64
GROUP = 8
ROOT_HALF = math.sqrt(0.5)


def unit(turns):
    return (math.cos(2.0 * math.pi * turns), math.sin(2.0 * math.pi * turns))


def plus(a, b):
    return (a[0] + b[0], a[1] + b[1])


def minus(a, b):
    return (a[0] - b[0], a[1] - b[1])


def turn(a, turns):
    turns = turns % 1.0
    if turns == 0.0:
        return a
    c, s = unit(turns)
    return (a[0] * c - a[1] * s, a[1] * c + a[0] * s)


def quarter(a, sign):
    if sign > 0:
        return (-a[1], a[0])
    return (a[1], -a[0])


def dft4(v, sign):
    t0, t1 = plus(v[0], v[2]), minus(v[0], v[2])
    t2, t3 = plus(v[1], v[3]), quarter(minus(v[1], v[3]), sign)
    return [plus(t0, t2), plus(t1, t3), minus(t0, t2), minus(t1, t3)]


def dft8(v, sign):
    up = [plus(v[n], v[n + 4]) for n in range(4)]
    down = [minus(v[n], v[n + 4]) for n in range(4)]
    r, i = down[1]
    down[1] = ((r - sign * i) * ROOT_HALF, (i + sign * r) * ROOT_HALF)
    down[2] = quarter(down[2], sign)
    r, i = down[3]
    down[3] = ((-r - sign * i) * ROOT_HALF, (sign * r - i) * ROOT_HALF)
    even, odd = dft4(up, sign), dft4(down, sign)
    return [even[k // 2] if k % 2 == 0 else odd[k // 2] for k in range(8)]


def load_pair(ref, *at):
    return (ref[(*at, slice(None), slice(0, LANES))], ref[(*at, slice(None), slice(LANES, 2 * LANES))])


def store_pair(ref, pair, *at):
    ref[(*at, slice(None), slice(0, LANES))] = pair[0]
    ref[(*at, slice(None), slice(LANES, 2 * LANES))] = pair[1]


def three_pass(rows, table):
    high = rows.astype(jnp.bfloat16)
    low = (rows - high.astype(jnp.float32)).astype(jnp.bfloat16)
    return jnp.dot(
        jnp.concatenate([high, low, high], axis=1), table, preferred_element_type=jnp.float32
    )


def forward_kernel(signal, cotangent, long_filter, phases, table, out, first, second):
    for number, source in enumerate((long_filter, signal, cotangent)):
        for b in range(8):
            column = []
            for a in range(8):
                x = source[:, (8 * a + b) * LANES : (8 * a + b + 1) * LANES]
                c, s = unit(-a / 32.0)
                column.append((x * c, x * s))
            for q, value in enumerate(dft8(column, -1)):
                store_pair(first, turn(value, -b * (q + 0.25) / 64.0), 8 * b + q)
        for q in range(8):
            column = [load_pair(first, 8 * b + q) for b in range(8)]
            for p, (r, i) in enumerate(dft8(column, -1)):
                at = q + 8 * p
                c = phases[at : at + 1, :LANES]
                s = phases[at : at + 1, LANES:]
                rows = slice(GROUP * number, GROUP * (number + 1))
                second[at, rows, :LANES] = r * c + i * s
                second[at, rows, LANES:] = i * c - r * s
    step = 8
    for at in range(0, OUTER, step):
        rows = second[at : at + step].reshape(step * 3 * GROUP, 2 * LANES)
        out[at : at + step] = three_pass(rows, table[...]).reshape(step, 3, GROUP, 2 * LANES)


def middle_kernel(spread, out, first, spectra):
    scale = 1.0 / (128.0 * 8192.0)

    def transform(number, half):
        shift = 0.5 * half
        for b in range(8):
            column = [
                turn(load_pair(spread, 8 * a + b, number), -a * shift / 8.0) for a in range(8)
            ]
            for q, value in enumerate(dft8(column, -1)):
                store_pair(first, turn(value, -b * (q + shift) / 64.0), 8 * b + q)
        for q in range(8):
            column = [load_pair(first, 8 * b + q) for b in range(8)]
            for p, value in enumerate(dft8(column, -1)):
                store_pair(spectra, value, number, q + 8 * p)

    for half in range(2):
        for number in range(3):
            transform(number, half)
        for at in range(OUTER):
            c, s = unit((2 * at + half) / 128.0)
            c, s = (1.0 + s) * scale, -c * scale
            r, i = load_pair(spectra, 2, at)
            r, i = r * c - i * s, i * c + r * s
            for number in range(2):
                fr, fi = load_pair(spectra, number, at)
                store_pair(spectra, (r * fr + i * fi, i * fr - r * fi), number, at)
        for number in range(2):
            for q in range(8):
                column = [load_pair(spectra, number, q + 8 * p) for p in range(8)]
                for b, value in enumerate(dft8(column, 1)):
                    store_pair(first, turn(value, b * q / 64.0), 8 * b + q)
            for b in range(8):
                column = [load_pair(first, 8 * b + q) for q in range(8)]
                for a, value in enumerate(dft8(column, 1)):
                    at = 8 * a + b
                    if half:
                        value = plus(load_pair(out, at, number), turn(value, at / 128.0))
                    store_pair(out, value, at, number)


def inverse_kernel(returned, phases, table, grad_signal, grad_filter, first, second):
    step = 8
    for at in range(0, OUTER, step):
        rows = returned[at : at + step].reshape(step * 2 * GROUP, 2 * LANES)
        second[at : at + step] = three_pass(rows, table[...]).reshape(step, 2, GROUP, 2 * LANES)
    for number, target in enumerate((grad_signal, grad_filter)):
        for q in range(8):
            column = []
            for p in range(8):
                at = q + 8 * p
                r, i = load_pair(second, at, number)
                c = phases[at : at + 1, :LANES]
                s = phases[at : at + 1, LANES:]
                column.append((r * c - i * s, i * c + r * s))
            for b, value in enumerate(dft8(column, 1)):
                store_pair(first, turn(value, b * (q + 0.25) / 64.0), 8 * b + q)
        for b in range(8):
            column = [load_pair(first, 8 * b + q) for q in range(8)]
            for a, (r, i) in enumerate(dft8(column, 1)):
                c, s = unit(a / 32.0)
                at = (8 * a + b) * LANES
                target[:, at : at + LANES] = r * c - i * s


def phase_table():
    turns = np.arange(LANES)[None, :] * (np.arange(OUTER)[:, None] + 0.25) / 8192.0
    angle = 2.0 * np.pi * turns
    return np.concatenate([np.cos(angle), np.sin(angle)], axis=1).astype(np.float32)


def section_table(inverse):
    angle = 2.0 * np.pi * (np.outer(np.arange(LANES), np.arange(LANES)) % LANES) / LANES
    c, s = np.cos(angle), np.sin(angle)
    whole = np.block([[c, -s], [s, c]])
    if inverse:
        whole = whole.T
    high = whole.astype(np.float32).astype(ml_dtypes.bfloat16)
    low = (whole - high.astype(np.float64)).astype(np.float32).astype(ml_dtypes.bfloat16)
    return np.concatenate([high, high, low], axis=0)


def whole_block(shape):
    return pl.BlockSpec(shape, lambda g: (0,) * len(shape))


PARAMS = pltpu.CompilerParams(vmem_limit_bytes=40 * 1024 * 1024)


def forward(signal, cotangent, long_filter):
    channels = signal.shape[0]
    rows = pl.BlockSpec((GROUP, OUTER * LANES), lambda g: (g, 0))
    return pl.pallas_call(
        forward_kernel,
        grid=(channels // GROUP,),
        in_specs=[rows] * 3 + [whole_block((OUTER, 2 * LANES)), whole_block((6 * LANES, 2 * LANES))],
        out_specs=pl.BlockSpec((OUTER, 3, GROUP, 2 * LANES), lambda g: (0, 0, g, 0)),
        out_shape=jax.ShapeDtypeStruct((OUTER, 3, channels, 2 * LANES), jnp.float32),
        scratch_shapes=[
            pltpu.VMEM((OUTER, GROUP, 2 * LANES), jnp.float32),
            pltpu.VMEM((OUTER, 3 * GROUP, 2 * LANES), jnp.float32),
        ],
        compiler_params=PARAMS,
        name="forward",
    )(signal, cotangent, long_filter, phase_table(), section_table(False))


def middle(spread):
    channels = spread.shape[2]
    return pl.pallas_call(
        middle_kernel,
        grid=(channels // GROUP,),
        in_specs=[pl.BlockSpec((OUTER, 3, GROUP, 2 * LANES), lambda g: (0, 0, g, 0))],
        out_specs=pl.BlockSpec((OUTER, 2, GROUP, 2 * LANES), lambda g: (0, 0, g, 0)),
        out_shape=jax.ShapeDtypeStruct((OUTER, 2, channels, 2 * LANES), jnp.float32),
        scratch_shapes=[
            pltpu.VMEM((OUTER, GROUP, 2 * LANES), jnp.float32),
            pltpu.VMEM((3, OUTER, GROUP, 2 * LANES), jnp.float32),
        ],
        compiler_params=PARAMS,
        name="middle",
    )(spread)


def inverse(returned):
    channels = returned.shape[2]
    rows = pl.BlockSpec((GROUP, OUTER * LANES), lambda g: (g, 0))
    result = jax.ShapeDtypeStruct((channels, OUTER * LANES), jnp.float32)
    return pl.pallas_call(
        inverse_kernel,
        grid=(channels // GROUP,),
        in_specs=[
            pl.BlockSpec((OUTER, 2, GROUP, 2 * LANES), lambda g: (0, 0, g, 0)),
            whole_block((OUTER, 2 * LANES)),
            whole_block((6 * LANES, 2 * LANES)),
        ],
        out_specs=[rows, rows],
        out_shape=[result, result],
        scratch_shapes=[
            pltpu.VMEM((OUTER, GROUP, 2 * LANES), jnp.float32),
            pltpu.VMEM((OUTER, 2, GROUP, 2 * LANES), jnp.float32),
        ],
        compiler_params=PARAMS,
        name="inverse",
    )(returned, phase_table(), section_table(True))


def exchange(blocks):
    sizes = blocks.shape
    flat = blocks.reshape(sizes[0], sizes[1] * sizes[2], sizes[3])
    moved = lax.all_to_all(flat, ("seqo", "seqi"), split_axis=0, concat_axis=0, tiled=True)
    return moved.reshape(sizes)


def on_device(signal, cotangent, long_filter):
    spread = exchange(forward(signal, cotangent, long_filter))
    grad_signal, grad_filter = inverse(exchange(middle(spread)))
    return grad_signal, grad_filter


def solution(mesh):
    spec = P("chan", ("seqo", "seqi"))
    return jax.shard_map(
        on_device, mesh=mesh, in_specs=(spec,) * 3, out_specs=(spec,) * 2, check_vma=False
    )
```

profile of v0, /device:TPU:1, one launch (start us, length us, event | category | flops | bytes accessed | tf_op | source)
XLA Modules:
  0.0 141.0 jit_solution(5193417778032103134)
XLA Ops:
  0.6 0.0 copy-start
  0.6 1.1 copy-done
  1.8 0.0 copy-start.1
  1.8 1.1 copy-done.1
  2.9 0.0 copy-start.2
  2.9 1.1 copy-done.2
  4.0 0.0 copy-start.3
  4.0 1.0 copy-done.3
  5.0 0.0 copy-start.5
  5.0 0.8 copy-done.5
  5.9 4.6 %forward.1 = f32[64,3,24,256]{3,2,1,0:T(8,128)S(1)} custom-call(f32[24,8192]{1,0:T(8,128)S(1)} %copy-done, f32[24,8192]{1,0:T(8,128)S(1)} %copy-done.1, f32[24,8192]{1,0:T(8,128)S(1)} %copy-done.2, f32[64,256]{1,0:T(8,128)S(1)} %copy-done.5, bf16[768,256]{1,0:T(8,128)(2,1)S(1)} %copy-done.3), custom_call_target="tpu_custom_call" | custom-call | tf_op jit(solution)/shard_map/forward/pallas_call | solution.py:197
  10.5 71.5 %all_to_all.10 = f32[64,72,256]{2,1,0:T(8,128)S(1)} all-to-all(f32[64,72,256]{2,1,0:T(8,128)S(1)} %bitcast.4), channel_id=1, replica_groups=mesh['seqo'=4,'seqi'=16,'chan'=2] {'seqo','seqi'}, dimensions={0} | all-to-all | bytes 9437184 | tf_op jit(solution)/shard_map/all_to_all | solution.py:255
  82.0 7.8 %middle.1 = f32[64,2,24,256]{3,2,1,0:T(8,128)S(1)} custom-call(f32[64,3,24,256]{3,2,1,0:T(8,128)S(1)} %bitcast.5), custom_call_target="tpu_custom_call" | custom-call | tf_op jit(solution)/shard_map/middle/pallas_call | solution.py:214
  89.8 0.0 copy-start.4
  89.8 0.0 copy-start.6
  89.8 47.3 %all_to_all.11 = f32[64,48,256]{2,1,0:T(8,128)S(1)} all-to-all(f32[64,48,256]{2,1,0:T(8,128)S(1)} %bitcast.7), channel_id=1, replica_groups=mesh['seqo'=4,'seqi'=16,'chan'=2] {'seqo','seqi'}, dimensions={0} | all-to-all | bytes 6291456 | tf_op jit(solution)/shard_map/all_to_all | solution.py:255
  137.1 0.0 copy-done.4
  137.1 0.0 copy-done.6
  137.1 3.9 %inverse.1 = (f32[24,8192]{1,0:T(8,128)}, f32[24,8192]{1,0:T(8,128)}) custom-call(f32[64,2,24,256]{3,2,1,0:T(8,128)S(1)} %bitcast.6, f32[64,256]{1,0:T(8,128)S(1)} %copy-done.6, bf16[768,256]{1,0:T(8,128)(2,1)S(1)} %copy-done.4), custom_call_target="tpu_custom_call" | custom-call | tf_op jit(solution)/shard_map/inverse/pallas_call | solution.py:233
Async XLA Ops:
  0.6 1.1 copy-start
  1.8 1.1 copy-start.1
  2.9 1.1 copy-start.2
  4.0 1.0 copy-start.3
  5.0 0.8 copy-start.5
  89.8 47.3 %copy-start.4 = (bf16[768,256]{1,0:T(8,128)(2,1)S(1)}, bf16[768,256]{1,0:T(8,128)(2,1)}, u32[]{:S(2)}) copy-start(bf16[768,256]{1,0:T(8,128)(2,1)} %constant.8.clone.table) | copy-start | bytes 1179652
  89.8 47.3 %copy-start.6 = (f32[64,256]{1,0:T(8,128)S(1)}, f32[64,256]{1,0:T(8,128)}, u32[]{:S(2)}) copy-start(f32[64,256]{1,0:T(8,128)} %constant.6.clone.phases) | copy-start | bytes 196612
where the time goes:
time: 141 us
  blocking collectives  119 us (84%)
  Pallas kernels  16.3 us (12%)
  local copies, waits for them, and re-layouts  5.24 us (4%)
    all_to_all x2, blocking collectives, exchange(): lax.all_to_all(flat, ('seqo', 'seqi'), split_axis=0, concat_axis=0, tiled...  119 us
    pallas_call x1, Pallas kernels, middle(): pl.pallas_call(middle_kernel, grid=(channels // GROUP,), in_specs=[pl.Blo...  7.77 us
    unnamed x14, local copies, waits for them, and re-layouts  5.24 us
    pallas_call x1, Pallas kernels, forward(): pl.pallas_call(forward_kernel, grid=(channels // GROUP,), in_specs=[rows]...  4.63 us
    pallas_call x1, Pallas kernels, inverse(): pl.pallas_call(inverse_kernel, grid=(channels // GROUP,), in_specs=[pl.Bl...  3.91 us

commit v1 on v0

v1 whole, which is shorter than its diff:
```python
import math

import jax
import jax.numpy as jnp
import ml_dtypes
import numpy as np
from jax import lax
from jax.experimental import pallas as pl
from jax.experimental.pallas import tpu as pltpu
from jax.sharding import PartitionSpec as P

LANES = 128
BLOCKS = 64
ROWS = 64
TILE = 8
TILES = ROWS // TILE
HALF_TILES = TILES // 2
LENGTH = BLOCKS * ROWS * LANES
ROOT_HALF = math.sqrt(0.5)


def unit(turns):
    return (math.cos(2.0 * math.pi * turns), math.sin(2.0 * math.pi * turns))


def plus(a, b):
    return (a[0] + b[0], a[1] + b[1])


def minus(a, b):
    return (a[0] - b[0], a[1] - b[1])


def turn(a, turns):
    turns = turns % 1.0
    if turns == 0.0:
        return a
    c, s = unit(turns)
    return (a[0] * c - a[1] * s, a[1] * c + a[0] * s)


def quarter(a, sign):
    if sign > 0:
        return (-a[1], a[0])
    return (a[1], -a[0])


def dft4(v, sign):
    t0, t1 = plus(v[0], v[2]), minus(v[0], v[2])
    t2, t3 = plus(v[1], v[3]), quarter(minus(v[1], v[3]), sign)
    return [plus(t0, t2), plus(t1, t3), minus(t0, t2), minus(t1, t3)]


def dft8(v, sign):
    up = [plus(v[n], v[n + 4]) for n in range(4)]
    down = [minus(v[n], v[n + 4]) for n in range(4)]
    r, i = down[1]
    down[1] = ((r - sign * i) * ROOT_HALF, (i + sign * r) * ROOT_HALF)
    down[2] = quarter(down[2], sign)
    r, i = down[3]
    down[3] = ((-r - sign * i) * ROOT_HALF, (sign * r - i) * ROOT_HALF)
    even, odd = dft4(up, sign), dft4(down, sign)
    return [even[k // 2] if k % 2 == 0 else odd[k // 2] for k in range(8)]


def load_pair(ref, at):
    return (ref[at, :, :LANES], ref[at, :, LANES:])


def store_pair(ref, pair, at):
    ref[at, :, :LANES] = pair[0]
    ref[at, :, LANES:] = pair[1]


def split(rows):
    high = rows.astype(jnp.bfloat16)
    return high, (rows - high.astype(jnp.float32)).astype(jnp.bfloat16)


def times_right(rows, table):
    high, low = split(rows)
    return jnp.dot(
        jnp.concatenate([high, low, high], axis=1), table, preferred_element_type=jnp.float32
    )


def times_left(table, columns):
    high, low = split(columns)
    return jnp.dot(
        table, jnp.concatenate([high, high, low], axis=0), preferred_element_type=jnp.float32
    )


def pack_kernel(signal, cotangent, long_filter, out):
    step = pl.program_id(0)

    @pl.when(step < pl.num_programs(0) - 1)
    def _():
        for u in range(TILES):
            at = slice(TILE * u, TILE * (u + 1))
            for source, core in ((long_filter, 0), (signal, 1), (cotangent, None)):
                slabs = [
                    source[:, (TILE * u + v) * LANES : (TILE * u + v + 1) * LANES]
                    for v in range(TILE)
                ]
                turned = jnp.swapaxes(jnp.stack(slabs), 0, 1)
                if core is None:
                    low = ROWS + TILE * (u % HALF_TILES)
                    out[:, u // HALF_TILES, low : low + TILE] = turned
                else:
                    out[:, core, at] = turned

    @pl.when(step == pl.num_programs(0) - 1)
    def _():
        out[...] = jnp.zeros(out.shape, out.dtype)


def unpack_kernel(landed, grad_signal, grad_filter):
    for core, target in ((0, grad_signal), (1, grad_filter)):
        for u in range(TILES):
            turned = jnp.swapaxes(landed[:, core, TILE * u : TILE * (u + 1)], 0, 1)
            for v in range(TILE):
                at = (TILE * u + v) * LANES
                target[:, at : at + LANES] = turned[v]


def correlate_kernel(
    core, own, near, far, phases, left, left_back, inner, right, right_back, out, first, spectra, back
):
    step = pl.program_id(0)

    def spread_blocks(source, number, tile):
        rows = pl.ds(pl.multiple_of(tile * TILE, TILE), TILE)
        for b in range(8):
            column = []
            for a in range(8):
                c, s = unit(-a / 32.0)
                x = source[8 * a + b]
                column.append((x * c, x * s))
            for q, value in enumerate(dft8(column, -1)):
                store_pair(first, turn(value, -b * (q + 0.25) / 64.0), 8 * b + q)
        for q in range(8):
            column = [load_pair(first, 8 * b + q) for b in range(8)]
            for p, (r, i) in enumerate(dft8(column, -1)):
                at = q + 8 * p
                c, s = load_pair(phases, at)
                spectra[at, number, rows, :LANES] = r * c + i * s
                spectra[at, number, rows, LANES:] = i * c - r * s

    @pl.when(step < TILES)
    def _():
        spread_blocks(own, 0, (step + HALF_TILES * core[0]) % TILES)

    @pl.when(step < HALF_TILES)
    def _():
        spread_blocks(near, 1, (step + HALF_TILES * core[0]) % TILES)

    @pl.when((step >= HALF_TILES) & (step < TILES))
    def _():
        spread_blocks(far, 1, (step + HALF_TILES * core[0]) % TILES)

    @pl.when(step == TILES)
    def _():
        batch = 2
        c, s = inner[:, :LANES], inner[:, LANES:]

        def body(turn_number, carry):
            base = turn_number * batch
            columns = []
            for e in range(batch):
                for number in range(2):
                    x = spectra[base + e, number]
                    columns.append(jnp.concatenate([x[:, :LANES], x[:, LANES:]], axis=0))
            y = times_left(left[...], jnp.concatenate(columns, axis=1))
            rows = []
            for n in range(2 * batch):
                r = y[:ROWS, n * LANES : (n + 1) * LANES]
                i = y[ROWS:, n * LANES : (n + 1) * LANES]
                rows.append(jnp.concatenate([r * c + i * s, i * c - r * s], axis=1))
            z = times_right(jnp.concatenate(rows, axis=0), right[...])
            rows = []
            for e in range(batch):
                f = z[2 * e * ROWS : (2 * e + 1) * ROWS]
                g = z[(2 * e + 1) * ROWS : (2 * e + 2) * ROWS]
                fr, fi, gr, gi = f[:, :LANES], f[:, LANES:], g[:, :LANES], g[:, LANES:]
                rows.append(jnp.concatenate([gr * fr + gi * fi, gi * fr - gr * fi], axis=1))
            z = times_right(jnp.concatenate(rows, axis=0), right_back[...])
            columns = []
            for e in range(batch):
                r = z[e * ROWS : (e + 1) * ROWS, :LANES]
                i = z[e * ROWS : (e + 1) * ROWS, LANES:]
                columns.append(jnp.concatenate([r * c - i * s, i * c + r * s], axis=0))
            y = times_left(left_back[...], jnp.concatenate(columns, axis=1))
            for e in range(batch):
                back[base + e, :, :LANES] = y[:ROWS, e * LANES : (e + 1) * LANES]
                back[base + e, :, LANES:] = y[ROWS:, e * LANES : (e + 1) * LANES]
            return carry

        lax.fori_loop(0, BLOCKS // batch, body, 0)

    @pl.when(step > TILES)
    def _():
        rows = pl.ds(pl.multiple_of((step - TILES - 1) * TILE, TILE), TILE)
        scale = 1.0 / LENGTH
        for q in range(8):
            column = []
            for p in range(8):
                at = q + 8 * p
                r, i = back[at, rows, :LANES], back[at, rows, LANES:]
                c, s = load_pair(phases, at)
                column.append((r * c - i * s, i * c + r * s))
            for b, value in enumerate(dft8(column, 1)):
                store_pair(first, turn(value, b * (q + 0.25) / 64.0), 8 * b + q)
        for b in range(8):
            column = [load_pair(first, 8 * b + q) for q in range(8)]
            for a, (r, i) in enumerate(dft8(column, 1)):
                c, s = unit(a / 32.0)
                out[8 * a + b] = r * (c * scale) - i * (s * scale)


def side_by_side(turns):
    angle = 2.0 * np.pi * turns
    return np.concatenate([np.cos(angle), np.sin(angle)], axis=-1).astype(np.float32)


def outer_phases():
    position = np.arange(ROWS * LANES).reshape(1, ROWS, LANES)
    return side_by_side(position * (np.arange(BLOCKS).reshape(BLOCKS, 1, 1) + 0.25) / LENGTH)


def inner_phases():
    return side_by_side(np.outer(np.arange(ROWS), np.arange(LANES)) / (ROWS * LANES))


def halves(whole):
    high = whole.astype(np.float32).astype(ml_dtypes.bfloat16)
    low = (whole - high.astype(np.float64)).astype(np.float32).astype(ml_dtypes.bfloat16)
    return high, low


def rotation(size, inverse):
    angle = 2.0 * np.pi * (np.outer(np.arange(size), np.arange(size)) % size) / size
    c, s = np.cos(angle), np.sin(angle)
    whole = np.block([[c, s], [-s, c]])
    return whole.T if inverse else whole


def left_table(inverse):
    high, low = halves(rotation(ROWS, inverse))
    return np.concatenate([high, low, high], axis=1)


def right_table(inverse):
    high, low = halves(rotation(LANES, inverse).T)
    return np.concatenate([high, high, low], axis=0)


PARAMS = pltpu.CompilerParams(vmem_limit_bytes=56 * 1024 * 1024)


def pack(signal, cotangent, long_filter, chips):
    channels = signal.shape[0]
    groups = channels // TILE
    rows = pl.BlockSpec((TILE, ROWS * LANES), lambda g: (jnp.minimum(g, groups - 1), 0))
    height = ROWS + ROWS // 2
    return pl.pallas_call(
        pack_kernel,
        grid=(chips // TILE,),
        in_specs=[rows] * 3,
        out_specs=pl.BlockSpec((TILE, 2, height, LANES), lambda g: (g, 0, 0, 0)),
        out_shape=jax.ShapeDtypeStruct((chips, 2, height, LANES), jnp.float32),
        compiler_params=PARAMS,
        name="pack",
    )(signal, cotangent, long_filter)


def unpack(landed, channels):
    rows = pl.BlockSpec((TILE, ROWS * LANES), lambda g: (g, 0))
    result = jax.ShapeDtypeStruct((channels, ROWS * LANES), jnp.float32)
    return pl.pallas_call(
        unpack_kernel,
        grid=(channels // TILE,),
        in_specs=[pl.BlockSpec((TILE, 2, ROWS, LANES), lambda g: (g, 0, 0, 0))],
        out_specs=[rows, rows],
        out_shape=[result, result],
        compiler_params=PARAMS,
        name="unpack",
    )(landed)


def correlate(core, arrived, swapped):
    last = TILES - 1

    def whole_block(table):
        return pl.BlockSpec(table.shape, lambda i, c: (0,) * table.ndim)

    def tile_of(i, c):
        return (i + HALF_TILES * c[0]) % TILES

    def phase_at(i, c):
        return (0, jnp.where(i < TILES, tile_of(i, c), jnp.maximum(i - TILES - 1, 0)), 0)

    tables = [
        left_table(False),
        left_table(True),
        inner_phases(),
        right_table(False),
        right_table(True),
    ]
    tile = (BLOCKS, TILE, LANES)
    return pl.pallas_call(
        correlate_kernel,
        grid_spec=pltpu.PrefetchScalarGridSpec(
            num_scalar_prefetch=1,
            grid=(2 * TILES + 1,),
            in_specs=[
                pl.BlockSpec(tile, lambda i, c: (0, tile_of(jnp.minimum(i, last), c), 0)),
                pl.BlockSpec(tile, lambda i, c: (0, TILES + jnp.minimum(i, HALF_TILES - 1), 0)),
                pl.BlockSpec(tile, lambda i, c: (0, jnp.clip(i - HALF_TILES, 0, HALF_TILES - 1), 0)),
                pl.BlockSpec((BLOCKS, TILE, 2 * LANES), phase_at),
            ]
            + [whole_block(table) for table in tables],
            out_specs=pl.BlockSpec(tile, lambda i, c: (0, jnp.maximum(i - TILES - 1, 0), 0)),
            scratch_shapes=[
                pltpu.VMEM((BLOCKS, TILE, 2 * LANES), jnp.float32),
                pltpu.VMEM((BLOCKS, 2, ROWS, 2 * LANES), jnp.float32),
                pltpu.VMEM((BLOCKS, ROWS, 2 * LANES), jnp.float32),
            ],
        ),
        out_shape=jax.ShapeDtypeStruct((BLOCKS, ROWS, LANES), jnp.float32),
        compiler_params=PARAMS,
        name="correlate",
    )(core, arrived, arrived, swapped, outer_phases(), *tables)


def exchange(blocks):
    return lax.all_to_all(blocks, ("seqo", "seqi"), split_axis=0, concat_axis=0, tiled=True)


def on_device(signal, cotangent, long_filter):
    channels = signal.shape[0]
    inner = lax.axis_size("seqi")
    members = lax.axis_size("seqo") * inner
    packed = pack(signal, cotangent, long_filter, members // 2)
    arrived = exchange(packed.reshape(members, *packed.shape[2:]))
    swapped = lax.ppermute(arrived[:, ROWS:], "seqi", [(n, n ^ 1) for n in range(inner)])
    core = (lax.axis_index("seqi") % 2).astype(jnp.int32).reshape(1)
    landed = exchange(correlate(core, arrived, swapped))
    return tuple(unpack(landed.reshape(members // 2, 2, ROWS, LANES), channels))


def solution(mesh):
    spec = P("chan", ("seqo", "seqi"))
    return jax.shard_map(
        on_device, mesh=mesh, in_specs=(spec,) * 3, out_specs=(spec,) * 2, check_vma=False
    )
```

time: 141 us -> 149 us (1.057)
  Pallas kernels: 16.3 us -> 52.6 us
  blocking collectives: 119 us -> 91.2 us
  local copies, waits for them, and re-layouts: 5.24 us -> 1.11 us
  waiting for transfers between devices: 0 us -> 2.63 us
    pallas_call x3, Pallas kernels: 16.3 us -> 52.6 us  [the longest x1 44.9 us: correlate(): pl.pallas_call(correlate_kernel, grid_spec=pltpu.PrefetchScalarGridSpec(n...]
    all_to_all x2, blocking collectives: 119 us -> 91.2 us  [exchange(): lax.all_to_all(blocks, ('seqo', 'seqi'), split_axis=0, concat_axis=0, til...]
    unnamed x14 -> x2, local copies, waits for them, and re-layouts: 5.24 us -> 0.01 us
    ppermute x0 -> x1, waiting for transfers between devices: none -> 2.63 us  [on_device(): lax.ppermute(arrived[:, ROWS:], 'seqi', [(n, n ^ 1) for n in range(inner)])]
  transfers between devices with their start and end apart: 0 -> 1, of which waited for: 0 -> 1; matrix products, arithmetic and copies ran while one was open for 0% -> 0% of each run, Pallas kernels for 0% -> 0%
where the time goes in v1:
time: 149 us
  blocking collectives  91.2 us (61%)
  Pallas kernels  52.6 us (35%)
  waiting for transfers between devices  2.63 us (2%)
    all_to_all x2, blocking collectives, exchange(): lax.all_to_all(blocks, ('seqo', 'seqi'), split_axis=0, concat_axis=0, til...  91.2 us
    pallas_call x1, Pallas kernels, correlate(): pl.pallas_call(correlate_kernel, grid_spec=pltpu.PrefetchScalarGridSpec(n...  44.9 us
    pallas_call x1, Pallas kernels, pack(): pl.pallas_call(pack_kernel, grid=(chips // TILE,), in_specs=[rows] * 3, o...  4.26 us
    pallas_call x1, Pallas kernels, unpack(): pl.pallas_call(unpack_kernel, grid=(channels // TILE,), in_specs=[pl.Bloc...  3.38 us
  transfers between devices with their start and end apart: 1, of which 1 were waited for; matrix products, arithmetic and copies ran while one was open for 0% of the time, Pallas kernels for 0%

profile of v1, /device:TPU:1, one launch (start us, length us, event | category | flops | bytes accessed | tf_op | source)
XLA Modules:
  0.0 148.7 jit_solution(10279028566011626301)
XLA Ops:
  0.6 4.3 %pack.1 = f32[32,2,96,128]{3,2,1,0:T(8,128)} custom-call(f32[24,8192]{1,0:T(8,128)} %signal.1, f32[24,8192]{1,0:T(8,128)} %cotangent.1, f32[24,8192]{1,0:T(8,128)} %long_filter.1), custom_call_target="tpu_custom_call" | custom-call | tf_op jit(solution)/shard_map/pack/pallas_call | solution.py:266
  4.9 54.8 %all_to_all.10.own.near = f32[64,96,128]{2,1,0:T(8,128)S(1)} all-to-all(f32[64,96,128]{2,1,0:T(8,128)} %bitcast.3), channel_id=1, replica_groups=mesh['seqo'=4,'seqi'=16,'chan'=2] {'seqo','seqi'}, dimensions={0} | all-to-all | bytes 6291456 | tf_op jit(solution)/shard_map/all_to_all | solution.py:337
  59.7 0.0 copy-start
  59.7 1.1 slice.4
  60.8 0.6 collective-permute-start
  61.3 2.6 %collective-permute-done.far = f32[64,32,128]{2,1,0:T(8,128)} collective-permute-done((f32[64,32,128]{2,1,0:T(8,128)}, f32[64,32,128]{2,1,0:T(8,128)}, u32[]{:S(2)}, u32[]{:S(2)}) %collective-permute-start) | collective-permute-done | bytes 1048608 | tf_op jit(solution)/shard_map/ppermute | solution.py:346
  63.9 0.0 copy-done
  63.9 44.9 %correlate.1 = f32[64,64,128]{2,1,0:T(8,128)} custom-call(s32[1]{0:T(128)} %bitcast.core, f32[64,96,128]{2,1,0:T(8,128)} %copy-done, f32[64,96,128]{2,1,0:T(8,128)} %copy-done, f32[64,32,128]{2,1,0:T(8,128)} %collective-permute-done.far, f32[64,64,256]{2,1,0:T(8,128)} %constant.31.clone.phases, bf16[128,384]{1,0:T(8,128)(2,1)} %constant.32.clone.left, ...), custom_call_target="tpu_custom_call" | custom-call | tf_op jit(solution)/shard_map/correlate/pallas_call | solution.py:311
  108.9 36.4 %all_to_all.11 = f32[64,64,128]{2,1,0:T(8,128)} all-to-all(f32[64,64,128]{2,1,0:T(8,128)} %correlate.1), channel_id=1, replica_groups=mesh['seqo'=4,'seqi'=16,'chan'=2] {'seqo','seqi'}, dimensions={0} | all-to-all | bytes 4194304 | tf_op jit(solution)/shard_map/all_to_all | solution.py:337
  145.3 3.4 %unpack.1 = (f32[24,8192]{1,0:T(8,128)}, f32[24,8192]{1,0:T(8,128)}) custom-call(f32[32,2,64,128]{3,2,1,0:T(8,128)} %bitcast.4), custom_call_target="tpu_custom_call" | custom-call | tf_op jit(solution)/shard_map/unpack/pallas_call | solution.py:280
Async XLA Ops:
  59.7 4.3 %copy-start = (f32[64,96,128]{2,1,0:T(8,128)}, f32[64,96,128]{2,1,0:T(8,128)S(1)}, u32[]{:S(2)}) copy-start(f32[64,96,128]{2,1,0:T(8,128)S(1)} %all_to_all.10.own.near) | copy-start | bytes 9437188
  60.8 3.2 %collective-permute-start = (f32[64,32,128]{2,1,0:T(8,128)}, f32[64,32,128]{2,1,0:T(8,128)}, u32[]{:S(2)}, u32[]{:S(2)}) collective-permute-start(f32[64,32,128]{2,1,0:T(8,128)} %slice.4), channel_id=1, source_target_pairs={{0,2},{2,0},{4,6},{6,4},{8,10},{10,8},{12,14},{14,12},{16,18},{18,... | collective-permute-start | bytes 3145736 | tf_op jit(solution)/shard_map/ppermute | solution.py:346

commit v2 on v1

v2 whole, which is shorter than its diff:
```python
import math

import jax
import jax.numpy as jnp
import ml_dtypes
import numpy as np
from jax import lax
from jax.experimental import pallas as pl
from jax.experimental.pallas import tpu as pltpu
from jax.sharding import PartitionSpec as P

LANES = 128
BLOCKS = 64
ROWS = 64
TILE = 8
TILES = ROWS // TILE
HALF_TILES = TILES // 2
LENGTH = BLOCKS * ROWS * LANES
ROOT_HALF = math.sqrt(0.5)


def unit(turns):
    return (math.cos(2.0 * math.pi * turns), math.sin(2.0 * math.pi * turns))


def plus(a, b):
    return (a[0] + b[0], a[1] + b[1])


def minus(a, b):
    return (a[0] - b[0], a[1] - b[1])


def turn(a, turns):
    turns = turns % 1.0
    if turns == 0.0:
        return a
    c, s = unit(turns)
    return (a[0] * c - a[1] * s, a[1] * c + a[0] * s)


def quarter(a, sign):
    if sign > 0:
        return (-a[1], a[0])
    return (a[1], -a[0])


def dft4(v, sign):
    t0, t1 = plus(v[0], v[2]), minus(v[0], v[2])
    t2, t3 = plus(v[1], v[3]), quarter(minus(v[1], v[3]), sign)
    return [plus(t0, t2), plus(t1, t3), minus(t0, t2), minus(t1, t3)]


def dft8(v, sign):
    up = [plus(v[n], v[n + 4]) for n in range(4)]
    down = [minus(v[n], v[n + 4]) for n in range(4)]
    r, i = down[1]
    down[1] = ((r - sign * i) * ROOT_HALF, (i + sign * r) * ROOT_HALF)
    down[2] = quarter(down[2], sign)
    r, i = down[3]
    down[3] = ((-r - sign * i) * ROOT_HALF, (sign * r - i) * ROOT_HALF)
    even, odd = dft4(up, sign), dft4(down, sign)
    return [even[k // 2] if k % 2 == 0 else odd[k // 2] for k in range(8)]


def load_pair(ref, at):
    return (ref[at, :, :LANES], ref[at, :, LANES:])


def store_pair(ref, pair, at):
    ref[at, :, :LANES] = pair[0]
    ref[at, :, LANES:] = pair[1]


def split(rows):
    high = rows.astype(jnp.bfloat16)
    return high, (rows - high.astype(jnp.float32)).astype(jnp.bfloat16)


def times_right(rows, table):
    high, low = split(rows)
    return jnp.dot(
        jnp.concatenate([high, low, high], axis=1), table, preferred_element_type=jnp.float32
    )


def times_left(table, columns):
    high, low = split(columns)
    return jnp.dot(
        table, jnp.concatenate([high, high, low], axis=0), preferred_element_type=jnp.float32
    )


def pack_kernel(signal, cotangent, long_filter, out, taken, packed, in_sems, out_sems):
    groups = signal.shape[0] // TILE
    sources = (long_filter, signal, cotangent)

    def arrival(g, n):
        rows = pl.ds(TILE * g, TILE)
        return pltpu.make_async_copy(sources[n].at[rows], taken.at[g, n], in_sems.at[g, n])

    def departure(g, slot):
        return pltpu.make_async_copy(packed.at[g], out.at[pl.ds(TILE * slot, TILE)], out_sems.at[slot])

    for g in range(groups):
        for n in range(3):
            arrival(g, n).start()
    for g in range(groups):
        for n in range(3):
            arrival(g, n).wait()
        for u in range(TILES):
            for n in range(3):
                slabs = [
                    taken[g, n, :, (TILE * u + v) * LANES : (TILE * u + v + 1) * LANES]
                    for v in range(TILE)
                ]
                turned = jnp.swapaxes(jnp.stack(slabs), 0, 1)
                if n < 2:
                    packed[g, :, n, TILE * u : TILE * (u + 1)] = turned
                else:
                    low = ROWS + TILE * (u % HALF_TILES)
                    packed[g, :, u // HALF_TILES, low : low + TILE] = turned
        departure(g, g).start()
    for slot in range(groups, out.shape[0] // TILE):
        departure(groups - 1, slot).start()
    for slot in range(out.shape[0] // TILE):
        departure(min(slot, groups - 1), slot).wait()


def unpack_kernel(landed, grad_signal, grad_filter, taken, turned_out, in_sems, out_sems):
    groups = grad_signal.shape[0] // TILE
    targets = (grad_signal, grad_filter)

    def arrival(g):
        return pltpu.make_async_copy(landed.at[pl.ds(TILE * g, TILE)], taken.at[g], in_sems.at[g])

    def departure(g, n):
        rows = pl.ds(TILE * g, TILE)
        return pltpu.make_async_copy(turned_out.at[g, n], targets[n].at[rows], out_sems.at[g, n])

    for g in range(groups):
        arrival(g).start()
    for g in range(groups):
        arrival(g).wait()
        for n in range(2):
            for u in range(TILES):
                turned = jnp.swapaxes(taken[g, :, n, TILE * u : TILE * (u + 1)], 0, 1)
                for v in range(TILE):
                    at = (TILE * u + v) * LANES
                    turned_out[g, n, :, at : at + LANES] = turned[v]
            departure(g, n).start()
    for g in range(groups):
        for n in range(2):
            departure(g, n).wait()


def correlate_kernel(
    core,
    arrived,
    swapped,
    *refs,
):
    tables, out, copies = refs[:7], refs[7], refs[8:15]
    phases, lifts, left, left_back, inner, right, right_back = copies
    own, other, first, spectra, back, results, own_sems, other_sems, table_sems, out_sems = refs[15:]
    offset = HALF_TILES * core[0]

    def tile_rows(tile):
        return pl.ds(pl.multiple_of(tile * TILE, TILE), TILE)

    def own_copy(i):
        rows = tile_rows((i + offset) % TILES)
        return pltpu.make_async_copy(arrived.at[:, rows], own.at[i], own_sems.at[i])

    def other_copy(i):
        if i < HALF_TILES:
            source = arrived.at[:, pl.ds(ROWS + TILE * i, TILE)]
        else:
            source = swapped.at[:, pl.ds(TILE * (i - HALF_TILES), TILE)]
        return pltpu.make_async_copy(source, other.at[i], other_sems.at[i])

    def table_copy(n):
        return pltpu.make_async_copy(tables[n], copies[n], table_sems.at[n])

    def out_copy(i):
        return pltpu.make_async_copy(results.at[i], out.at[:, tile_rows(i)], out_sems.at[i])

    table_copy(0).start()
    table_copy(1).start()
    for i in range(TILES):
        own_copy(i).start()
        other_copy(i).start()
    for n in range(2, 7):
        table_copy(n).start()

    def lift(a, tile, at, sign):
        c, s = lifts[tile, at : at + 1, :LANES], lifts[tile, at : at + 1, LANES:]
        if sign > 0:
            return (a[0] * c - a[1] * s, a[1] * c + a[0] * s)
        return (a[0] * c + a[1] * s, a[1] * c - a[0] * s)

    def spread_blocks(source, i, number):
        tile = (i + offset) % TILES
        rows = tile_rows(tile)
        for b in range(8):
            column = []
            for a in range(8):
                c, s = unit(-a / 32.0)
                x = source[i, 8 * a + b]
                column.append((x * c, x * s))
            for q, value in enumerate(dft8(column, -1)):
                store_pair(first, turn(value, -b * (q + 0.25) / 64.0), 8 * b + q)
        for q in range(8):
            column = [load_pair(first, 8 * b + q) for b in range(8)]
            for p, value in enumerate(dft8(column, -1)):
                at = q + 8 * p
                r, i_part = lift(value, tile, at, -1)
                c, s = load_pair(phases, at)
                spectra[at, number, rows, :LANES] = r * c + i_part * s
                spectra[at, number, rows, LANES:] = i_part * c - r * s

    table_copy(0).wait()
    table_copy(1).wait()

    def spread_step(i, carry):
        pltpu.make_async_copy(arrived.at[:, pl.ds(0, TILE)], own.at[i], own_sems.at[i]).wait()
        pltpu.make_async_copy(arrived.at[:, pl.ds(0, TILE)], other.at[i], other_sems.at[i]).wait()
        spread_blocks(own, i, 0)
        spread_blocks(other, i, 1)
        return carry

    lax.fori_loop(0, TILES, spread_step, 0)
    for n in range(2, 7):
        table_copy(n).wait()

    batch = 16
    c, s = inner[:, :LANES], inner[:, LANES:]

    def body(turn_number, carry):
        base = turn_number * batch
        columns = []
        for e in range(batch):
            for number in range(2):
                x = spectra[base + e, number]
                columns.append(jnp.concatenate([x[:, :LANES], x[:, LANES:]], axis=0))
        y = times_left(left[...], jnp.concatenate(columns, axis=1))
        rows = []
        for n in range(2 * batch):
            r = y[:ROWS, n * LANES : (n + 1) * LANES]
            i = y[ROWS:, n * LANES : (n + 1) * LANES]
            rows.append(jnp.concatenate([r * c + i * s, i * c - r * s], axis=1))
        z = times_right(jnp.concatenate(rows, axis=0), right[...])
        rows = []
        for e in range(batch):
            f = z[2 * e * ROWS : (2 * e + 1) * ROWS]
            g = z[(2 * e + 1) * ROWS : (2 * e + 2) * ROWS]
            fr, fi, gr, gi = f[:, :LANES], f[:, LANES:], g[:, :LANES], g[:, LANES:]
            rows.append(jnp.concatenate([gr * fr + gi * fi, gi * fr - gr * fi], axis=1))
        z = times_right(jnp.concatenate(rows, axis=0), right_back[...])
        columns = []
        for e in range(batch):
            r = z[e * ROWS : (e + 1) * ROWS, :LANES]
            i = z[e * ROWS : (e + 1) * ROWS, LANES:]
            columns.append(jnp.concatenate([r * c - i * s, i * c + r * s], axis=0))
        y = times_left(left_back[...], jnp.concatenate(columns, axis=1))
        for e in range(batch):
            back[base + e, :, :LANES] = y[:ROWS, e * LANES : (e + 1) * LANES]
            back[base + e, :, LANES:] = y[ROWS:, e * LANES : (e + 1) * LANES]
        return carry

    lax.fori_loop(0, BLOCKS // batch, body, 0)

    def gather_step(tile, carry):
        rows = tile_rows(tile)
        scale = 1.0 / LENGTH
        for q in range(8):
            column = []
            for p in range(8):
                at = q + 8 * p
                r, i = back[at, rows, :LANES], back[at, rows, LANES:]
                c, s = load_pair(phases, at)
                column.append(lift((r * c - i * s, i * c + r * s), tile, at, 1))
            for b, value in enumerate(dft8(column, 1)):
                store_pair(first, turn(value, b * (q + 0.25) / 64.0), 8 * b + q)
        for b in range(8):
            column = [load_pair(first, 8 * b + q) for q in range(8)]
            for a, (r, i) in enumerate(dft8(column, 1)):
                c, s = unit(a / 32.0)
                results[tile, 8 * a + b] = r * (c * scale) - i * (s * scale)
        out_copy(tile).start()
        return carry

    lax.fori_loop(0, TILES, gather_step, 0)
    for i in range(TILES):
        out_copy(i).wait()


def side_by_side(turns):
    angle = 2.0 * np.pi * turns
    return np.concatenate([np.cos(angle), np.sin(angle)], axis=-1).astype(np.float32)


def outer_phases():
    position = np.arange(TILE * LANES).reshape(1, TILE, LANES)
    return side_by_side(position * (np.arange(BLOCKS).reshape(BLOCKS, 1, 1) + 0.25) / LENGTH)


def tile_phases():
    start = TILE * LANES * np.arange(TILES).reshape(TILES, 1, 1)
    turns = start * (np.arange(BLOCKS).reshape(1, BLOCKS, 1) + 0.25) / LENGTH
    return side_by_side(np.broadcast_to(turns, (TILES, BLOCKS, LANES)))


def inner_phases():
    return side_by_side(np.outer(np.arange(ROWS), np.arange(LANES)) / (ROWS * LANES))


def halves(whole):
    high = whole.astype(np.float32).astype(ml_dtypes.bfloat16)
    low = (whole - high.astype(np.float64)).astype(np.float32).astype(ml_dtypes.bfloat16)
    return high, low


def rotation(size, inverse):
    angle = 2.0 * np.pi * (np.outer(np.arange(size), np.arange(size)) % size) / size
    c, s = np.cos(angle), np.sin(angle)
    whole = np.block([[c, s], [-s, c]])
    return whole.T if inverse else whole


def left_table(inverse):
    high, low = halves(rotation(ROWS, inverse))
    return np.concatenate([high, low, high], axis=1)


def right_table(inverse):
    high, low = halves(rotation(LANES, inverse).T)
    return np.concatenate([high, high, low], axis=0)


PARAMS = pltpu.CompilerParams(vmem_limit_bytes=56 * 1024 * 1024)


ANY = pl.BlockSpec(memory_space=pl.ANY)


def pack(signal, cotangent, long_filter, chips):
    groups = signal.shape[0] // TILE
    height = ROWS + ROWS // 2
    return pl.pallas_call(
        pack_kernel,
        in_specs=[ANY] * 3,
        out_specs=ANY,
        out_shape=jax.ShapeDtypeStruct((chips, 2, height, LANES), jnp.float32),
        scratch_shapes=[
            pltpu.VMEM((groups, 3, TILE, ROWS * LANES), jnp.float32),
            pltpu.VMEM((groups, TILE, 2, height, LANES), jnp.float32),
            pltpu.SemaphoreType.DMA((groups, 3)),
            pltpu.SemaphoreType.DMA((chips // TILE,)),
        ],
        compiler_params=PARAMS,
        name="pack",
    )(signal, cotangent, long_filter)


def unpack(landed, channels):
    groups = channels // TILE
    result = jax.ShapeDtypeStruct((channels, ROWS * LANES), jnp.float32)
    return pl.pallas_call(
        unpack_kernel,
        in_specs=[ANY],
        out_specs=[ANY, ANY],
        out_shape=[result, result],
        scratch_shapes=[
            pltpu.VMEM((groups, TILE, 2, ROWS, LANES), jnp.float32),
            pltpu.VMEM((groups, 2, TILE, ROWS * LANES), jnp.float32),
            pltpu.SemaphoreType.DMA((groups,)),
            pltpu.SemaphoreType.DMA((groups, 2)),
        ],
        compiler_params=PARAMS,
        name="unpack",
    )(landed)


def correlate(core, arrived, swapped):
    tables = [
        outer_phases(),
        tile_phases(),
        left_table(False),
        left_table(True),
        inner_phases(),
        right_table(False),
        right_table(True),
    ]
    tile = (TILES, BLOCKS, TILE, LANES)
    return pl.pallas_call(
        correlate_kernel,
        in_specs=[pl.BlockSpec(memory_space=pltpu.SMEM)] + [ANY] * (2 + len(tables)),
        out_specs=ANY,
        out_shape=jax.ShapeDtypeStruct((BLOCKS, ROWS, LANES), jnp.float32),
        scratch_shapes=[pltpu.VMEM(table.shape, table.dtype) for table in tables]
        + [
            pltpu.VMEM(tile, jnp.float32),
            pltpu.VMEM(tile, jnp.float32),
            pltpu.VMEM((BLOCKS, TILE, 2 * LANES), jnp.float32),
            pltpu.VMEM((BLOCKS, 2, ROWS, 2 * LANES), jnp.float32),
            pltpu.VMEM((BLOCKS, ROWS, 2 * LANES), jnp.float32),
            pltpu.VMEM(tile, jnp.float32),
            pltpu.SemaphoreType.DMA((TILES,)),
            pltpu.SemaphoreType.DMA((TILES,)),
            pltpu.SemaphoreType.DMA((len(tables),)),
            pltpu.SemaphoreType.DMA((TILES,)),
        ],
        compiler_params=PARAMS,
        name="correlate",
    )(core, arrived, swapped, *tables)


def exchange(blocks):
    return lax.all_to_all(blocks, ("seqo", "seqi"), split_axis=0, concat_axis=0, tiled=True)


def on_device(signal, cotangent, long_filter):
    channels = signal.shape[0]
    inner = lax.axis_size("seqi")
    members = lax.axis_size("seqo") * inner
    packed = pack(signal, cotangent, long_filter, members // 2)
    arrived = exchange(packed.reshape(members, *packed.shape[2:]))
    swapped = lax.ppermute(arrived[:, ROWS:], "seqi", [(n, n ^ 1) for n in range(inner)])
    core = (lax.axis_index("seqi") % 2).astype(jnp.int32).reshape(1)
    landed = exchange(correlate(core, arrived, swapped))
    return tuple(unpack(landed.reshape(members // 2, 2, ROWS, LANES), channels))


def solution(mesh):
    spec = P("chan", ("seqo", "seqi"))
    return jax.shard_map(
        on_device, mesh=mesh, in_specs=(spec,) * 3, out_specs=(spec,) * 2, check_vma=False
    )
```

time: 149 us -> 126 us (0.85)
  Pallas kernels: 52.6 us -> 29.7 us
    pallas_call x3, Pallas kernels: 52.6 us -> 29.7 us  [the longest x1 24.4 us: correlate(): pl.pallas_call(correlate_kernel, in_specs=[pl.BlockSpec(memory_space=pltp...]
where the time goes in v2:
time: 126 us
  blocking collectives  91.2 us (72%)
  Pallas kernels  29.7 us (24%)
  waiting for transfers between devices  2.63 us (2%)
    all_to_all x2, blocking collectives, exchange(): lax.all_to_all(blocks, ('seqo', 'seqi'), split_axis=0, concat_axis=0, til...  91.2 us
    pallas_call x1, Pallas kernels, correlate(): pl.pallas_call(correlate_kernel, in_specs=[pl.BlockSpec(memory_space=pltp...  24.4 us
    pallas_call x1, Pallas kernels, pack(): pl.pallas_call(pack_kernel, in_specs=[ANY] * 3, out_specs=ANY, out_shape=...  3.01 us
    ppermute x1, waiting for transfers between devices, on_device(): lax.ppermute(arrived[:, ROWS:], 'seqi', [(n, n ^ 1) for n in range(inner)])  2.63 us
  transfers between devices with their start and end apart: 1, of which 1 were waited for; matrix products, arithmetic and copies ran while one was open for 0% of the time, Pallas kernels for 0%

profile of v2, /device:TPU:1, one launch (start us, length us, event | category | flops | bytes accessed | tf_op | source)
XLA Modules:
  0.0 125.9 jit_solution(11184385081232478826)
XLA Ops:
  0.6 3.0 %pack.1 = f32[32,2,96,128]{3,2,1,0:T(8,128)} custom-call(f32[24,8192]{1,0:T(8,128)} %signal.1, f32[24,8192]{1,0:T(8,128)} %cotangent.1, f32[24,8192]{1,0:T(8,128)} %long_filter.1), custom_call_target="tpu_custom_call" | custom-call | tf_op jit(solution)/shard_map/pack/pallas_call | solution.py:350
  3.6 54.8 %all_to_all.10.arrived = f32[64,96,128]{2,1,0:T(8,128)S(1)} all-to-all(f32[64,96,128]{2,1,0:T(8,128)} %bitcast.3), channel_id=1, replica_groups=mesh['seqo'=4,'seqi'=16,'chan'=2] {'seqo','seqi'}, dimensions={0} | all-to-all | bytes 6291456 | tf_op jit(solution)/shard_map/all_to_all | solution.py:420
  58.4 0.0 copy-start
  58.4 1.1 slice.4
  59.5 0.6 collective-permute-start
  60.1 2.6 %collective-permute-done.swapped = f32[64,32,128]{2,1,0:T(8,128)} collective-permute-done((f32[64,32,128]{2,1,0:T(8,128)}, f32[64,32,128]{2,1,0:T(8,128)}, u32[]{:S(2)}, u32[]{:S(2)}) %collective-permute-start) | collective-permute-done | bytes 1048608 | tf_op jit(solution)/shard_map/ppermute | solution.py:429
  62.7 0.0 copy-done
  62.7 24.4 %correlate.1 = f32[64,64,128]{2,1,0:T(8,128)} custom-call(s32[1]{0:T(128)} %bitcast.core, f32[64,96,128]{2,1,0:T(8,128)} %copy-done, f32[64,32,128]{2,1,0:T(8,128)} %collective-permute-done.swapped, f32[64,8,256]{2,1,0:T(8,128)} %constant.33.clone.refs_0_, f32[8,64,256]{2,1,0:T(8,128)} %constant.34.clone.refs_1_, bf16[128,384]{1,0:T(8,128)(2,1)} %constant.35.clone.refs_2_, ...), custom_call_target="tpu_custom_call" | custom-call | tf_op jit(solution)/shard_map/correlate/pallas_call | solution.py:396
  87.1 36.5 %all_to_all.11 = f32[64,64,128]{2,1,0:T(8,128)} all-to-all(f32[64,64,128]{2,1,0:T(8,128)} %correlate.1), channel_id=1, replica_groups=mesh['seqo'=4,'seqi'=16,'chan'=2] {'seqo','seqi'}, dimensions={0} | all-to-all | bytes 4194304 | tf_op jit(solution)/shard_map/all_to_all | solution.py:420
  123.6 2.3 %unpack.1 = (f32[24,8192]{1,0:T(8,128)}, f32[24,8192]{1,0:T(8,128)}) custom-call(f32[32,2,64,128]{3,2,1,0:T(8,128)} %bitcast.4), custom_call_target="tpu_custom_call" | custom-call | tf_op jit(solution)/shard_map/unpack/pallas_call | solution.py:369
Async XLA Ops:
  58.4 4.3 %copy-start = (f32[64,96,128]{2,1,0:T(8,128)}, f32[64,96,128]{2,1,0:T(8,128)S(1)}, u32[]{:S(2)}) copy-start(f32[64,96,128]{2,1,0:T(8,128)S(1)} %all_to_all.10.arrived) | copy-start | bytes 9437188
  59.5 3.2 %collective-permute-start = (f32[64,32,128]{2,1,0:T(8,128)}, f32[64,32,128]{2,1,0:T(8,128)}, u32[]{:S(2)}, u32[]{:S(2)}) collective-permute-start(f32[64,32,128]{2,1,0:T(8,128)} %slice.4), channel_id=1, source_target_pairs={{0,2},{2,0},{4,6},{6,4},{8,10},{10,8},{12,14},{14,12},{16,18},{18,... | collective-permute-start | bytes 3145736 | tf_op jit(solution)/shard_map/ppermute | solution.py:429

commit v3 on v2

--- a/solution.py
+++ b/solution.py
@@ -15,6 +15,8 @@
 TILE = 8
 TILES = ROWS // TILE
 HALF_TILES = TILES // 2
+SIZE = 4
+STEPS = 8 // SIZE
 LENGTH = BLOCKS * ROWS * LANES
 ROOT_HALF = math.sqrt(0.5)
 
@@ -63,15 +65,6 @@
     return [even[k // 2] if k % 2 == 0 else odd[k // 2] for k in range(8)]
 
 
-def load_pair(ref, at):
-    return (ref[at, :, :LANES], ref[at, :, LANES:])
-
-
-def store_pair(ref, pair, at):
-    ref[at, :, :LANES] = pair[0]
-    ref[at, :, LANES:] = pair[1]
-
-
 def split(rows):
     high = rows.astype(jnp.bfloat16)
     return high, (rows - high.astype(jnp.float32)).astype(jnp.bfloat16)
@@ -86,9 +79,10 @@
 
 def times_left(table, columns):
     high, low = split(columns)
-    return jnp.dot(
-        table, jnp.concatenate([high, high, low], axis=0), preferred_element_type=jnp.float32
+    both = jnp.dot(
+        table, jnp.concatenate([high, low], axis=0), preferred_element_type=jnp.float32
     )
+    return both[: 2 * ROWS] + both[2 * ROWS :]
 
 
 def pack_kernel(signal, cotangent, long_filter, out, taken, packed, in_sems, out_sems):
@@ -154,136 +148,212 @@
             departure(g, n).wait()
 
 
-def correlate_kernel(
-    core,
-    arrived,
-    swapped,
-    *refs,
-):
-    tables, out, copies = refs[:7], refs[7], refs[8:15]
-    phases, lifts, left, left_back, inner, right, right_back = copies
-    own, other, first, spectra, back, results, own_sems, other_sems, table_sems, out_sems = refs[15:]
+def correlate_kernel(core, arrived, swapped, *refs):
+    tables, out, copies = refs[:4], refs[4], refs[5:9]
+    phases, left, inner, right = copies
+    own, other, spread, even, odd, even_back, odd_back, gathered, results = refs[9:18]
+    held_entered, held_multiplied, held_turned = refs[18:21]
+    own_sems, other_sems, table_sems, phase_sems, out_sems = refs[21:]
     offset = HALF_TILES * core[0]
 
     def tile_rows(tile):
+        if isinstance(tile, int):
+            return slice(tile * TILE, (tile + 1) * TILE)
         return pl.ds(pl.multiple_of(tile * TILE, TILE), TILE)
 
     def own_copy(i):
-        rows = tile_rows((i + offset) % TILES)
-        return pltpu.make_async_copy(arrived.at[:, rows], own.at[i], own_sems.at[i])
+        return pltpu.make_async_copy(arrived.at[:, pl.ds(TILE * i, TILE)], own.at[i], own_sems.at[i])
 
     def other_copy(i):
         if i < HALF_TILES:
             source = arrived.at[:, pl.ds(ROWS + TILE * i, TILE)]
         else:
             source = swapped.at[:, pl.ds(TILE * (i - HALF_TILES), TILE)]
-        return pltpu.make_async_copy(source, other.at[i], other_sems.at[i])
+        return pltpu.make_async_copy(source, other.at[(i + offset) % TILES], other_sems.at[i])
 
     def table_copy(n):
         return pltpu.make_async_copy(tables[n], copies[n], table_sems.at[n])
 
+    def phase_copy(q):
+        return pltpu.make_async_copy(tables[0].at[q], phases.at[q], phase_sems.at[q])
+
     def out_copy(i):
         return pltpu.make_async_copy(results.at[i], out.at[:, tile_rows(i)], out_sems.at[i])
 
-    table_copy(0).start()
-    table_copy(1).start()
     for i in range(TILES):
         own_copy(i).start()
         other_copy(i).start()
-    for n in range(2, 7):
+    for n in range(1, len(tables)):
         table_copy(n).start()
-
-    def lift(a, tile, at, sign):
-        c, s = lifts[tile, at : at + 1, :LANES], lifts[tile, at : at + 1, LANES:]
-        if sign > 0:
-            return (a[0] * c - a[1] * s, a[1] * c + a[0] * s)
-        return (a[0] * c + a[1] * s, a[1] * c - a[0] * s)
-
-    def spread_blocks(source, i, number):
-        tile = (i + offset) % TILES
-        rows = tile_rows(tile)
+    for q in range(8):
+        phase_copy(q).start()
+    for ref in (held_entered, held_multiplied, held_turned, even_back, odd_back):
+        ref[...] = jnp.zeros(ref.shape, ref.dtype)
+
+    def over_high(source, slot, number):
         for b in range(8):
             column = []
             for a in range(8):
                 c, s = unit(-a / 32.0)
-                x = source[i, 8 * a + b]
+                x = source[slot, 8 * a + b]
                 column.append((x * c, x * s))
             for q, value in enumerate(dft8(column, -1)):
-                store_pair(first, turn(value, -b * (q + 0.25) / 64.0), 8 * b + q)
-        for q in range(8):
-            column = [load_pair(first, 8 * b + q) for b in range(8)]
-            for p, value in enumerate(dft8(column, -1)):
-                at = q + 8 * p
-                r, i_part = lift(value, tile, at, -1)
-                c, s = load_pair(phases, at)
-                spectra[at, number, rows, :LANES] = r * c + i_part * s
-                spectra[at, number, rows, LANES:] = i_part * c - r * s
-
-    table_copy(0).wait()
-    table_copy(1).wait()
+                r, i = turn(value, -b * (q + 0.25) / 64.0)
+                spread[number, slot, 8 * b + q, :, :LANES] = r
+                spread[number, slot, 8 * b + q, :, LANES:] = i
 
     def spread_step(i, carry):
+        slot = (i + offset) % TILES
         pltpu.make_async_copy(arrived.at[:, pl.ds(0, TILE)], own.at[i], own_sems.at[i]).wait()
-        pltpu.make_async_copy(arrived.at[:, pl.ds(0, TILE)], other.at[i], other_sems.at[i]).wait()
-        spread_blocks(own, i, 0)
-        spread_blocks(other, i, 1)
+        over_high(own, i, 0)
+        pltpu.make_async_copy(arrived.at[:, pl.ds(0, TILE)], other.at[slot], other_sems.at[i]).wait()
+        over_high(other, slot, 1)
         return carry
 
     lax.fori_loop(0, TILES, spread_step, 0)
-    for n in range(2, 7):
+    for n in range(1, len(tables)):
         table_copy(n).wait()
-
-    batch = 16
-    c, s = inner[:, :LANES], inner[:, LANES:]
-
-    def body(turn_number, carry):
-        base = turn_number * batch
+    phase_copy(0).wait()
+
+    def over_low(q, tile, number, target):
+        rows = tile_rows(tile)
+        column = []
+        for b in range(8):
+            at = 8 * b + q
+            column.append((spread[number, tile, at, :, :LANES], spread[number, tile, at, :, LANES:]))
+        for p, (r, i) in enumerate(dft8(column, -1)):
+            c, s = phases[q, p, rows, :LANES], phases[q, p, rows, LANES:]
+            target[p, number, rows, :LANES] = r * c + i * s
+            target[p, number, rows, LANES:] = i * c - r * s
+
+    def back_low(q, tile, source):
+        rows = tile_rows(tile)
+        column = []
+        for p in range(8):
+            r, i = source[p, rows, :LANES], source[p, rows, LANES:]
+            c, s = phases[q, p, rows, :LANES], phases[q, p, rows, LANES:]
+            column.append((r * c - i * s, i * c + r * s))
+        for b, (r, i) in enumerate(dft8(column, 1)):
+            gathered[tile, 8 * b + q, :, :LANES] = r
+            gathered[tile, 8 * b + q, :, LANES:] = i
+
+    c_inner, s_inner = inner[:, :LANES], inner[:, LANES:]
+
+    def entry_columns(source, first_bin):
         columns = []
-        for e in range(batch):
+        for e in range(SIZE):
             for number in range(2):
-                x = spectra[base + e, number]
+                x = source[first_bin + e, number]
                 columns.append(jnp.concatenate([x[:, :LANES], x[:, LANES:]], axis=0))
-        y = times_left(left[...], jnp.concatenate(columns, axis=1))
+        return columns
+
+    def lanes(y, n):
+        at = slice(n * LANES, (n + 1) * LANES)
+        return y[:ROWS, at], y[ROWS:, at]
+
+    def entry_rows(y):
         rows = []
-        for n in range(2 * batch):
-            r = y[:ROWS, n * LANES : (n + 1) * LANES]
-            i = y[ROWS:, n * LANES : (n + 1) * LANES]
-            rows.append(jnp.concatenate([r * c + i * s, i * c - r * s], axis=1))
-        z = times_right(jnp.concatenate(rows, axis=0), right[...])
-        rows = []
-        for e in range(batch):
+        for n in range(2 * SIZE):
+            r, i = lanes(y, n)
+            rows.append(
+                jnp.concatenate(
+                    [r * c_inner + i * s_inner, i * c_inner - r * s_inner], axis=1
+                )
+            )
+        return jnp.concatenate(rows, axis=0)
+
+    def product_rows(z):
+        made = []
+        for e in range(SIZE):
             f = z[2 * e * ROWS : (2 * e + 1) * ROWS]
             g = z[(2 * e + 1) * ROWS : (2 * e + 2) * ROWS]
             fr, fi, gr, gi = f[:, :LANES], f[:, LANES:], g[:, :LANES], g[:, LANES:]
-            rows.append(jnp.concatenate([gr * fr + gi * fi, gi * fr - gr * fi], axis=1))
-        z = times_right(jnp.concatenate(rows, axis=0), right_back[...])
+            made.append(jnp.concatenate([gi * fr - gr * fi, gr * fr + gi * fi], axis=1))
+        return jnp.concatenate(made, axis=0)
+
+    def exit_columns(z):
         columns = []
-        for e in range(batch):
-            r = z[e * ROWS : (e + 1) * ROWS, :LANES]
-            i = z[e * ROWS : (e + 1) * ROWS, LANES:]
-            columns.append(jnp.concatenate([r * c - i * s, i * c + r * s], axis=0))
-        y = times_left(left_back[...], jnp.concatenate(columns, axis=1))
-        for e in range(batch):
-            back[base + e, :, :LANES] = y[:ROWS, e * LANES : (e + 1) * LANES]
-            back[base + e, :, LANES:] = y[ROWS:, e * LANES : (e + 1) * LANES]
+        for e in range(SIZE):
+            i = z[e * ROWS : (e + 1) * ROWS, :LANES]
+            r = z[e * ROWS : (e + 1) * ROWS, LANES:]
+            columns.append(
+                jnp.concatenate(
+                    [i * c_inner + r * s_inner, r * c_inner - i * s_inner], axis=0
+                )
+            )
+        return jnp.concatenate(columns, axis=1)
+
+    def leave(target, first_bin, y, start):
+        for e in range(SIZE):
+            i, r = lanes(y, start + e)
+            target[first_bin + e, :, :LANES] = r
+            target[first_bin + e, :, LANES:] = i
+
+    def advance(flight, source, first_bin, target, last_bin):
+        entered, multiplied, turned = flight
+        leave(target, last_bin, times_left(left[...], turned), 0)
+        turned = exit_columns(times_right(multiplied, right[...]))
+        multiplied = product_rows(times_right(entered, right[...]))
+        if source is not None:
+            columns = jnp.concatenate(entry_columns(source, first_bin), axis=1)
+            entered = entry_rows(times_left(left[...], columns))
+        return entered, multiplied, turned
+
+    def left_at(step):
+        return -((step - 3) // STEPS), (step - 3) % STEPS * SIZE
+
+    delay = next(ago for ago, at in map(left_at, range(STEPS)) if at + SIZE == 8)
+
+    def half(flight, now, q_next, then, q_last, backs):
+        per_step = 2 * TILES // STEPS
+        for step in range(STEPS):
+            ago, last_bin = left_at(step)
+            flight = advance(flight, now, step * SIZE, backs[ago % 2], last_bin)
+            for n in range(step * per_step, (step + 1) * per_step):
+                over_low(q_next, n // 2, n % 2, then)
+            if last_bin + SIZE == 8:
+                for tile in range(TILES):
+                    back_low(q_last, tile, backs[ago % 2])
+        return flight
+
+    for tile in range(TILES):
+        over_low(0, tile, 0, even)
+        over_low(0, tile, 1, even)
+
+    def pair_step(t, carry):
+        phase_copy(2 * t + 1).wait()
+
+        @pl.when(t < 3)
+        def _():
+            phase_copy(2 * t + 2).wait()
+
+        flight = held_entered[...], held_multiplied[...], held_turned[...]
+        last = jnp.maximum(2 * t - delay, 0)
+        flight = half(flight, even, 2 * t + 1, odd, last, (even_back, odd_back))
+        last = jnp.maximum(2 * t + 1 - delay, 0)
+        flight = half(flight, odd, jnp.minimum(2 * t + 2, 7), even, last, (odd_back, even_back))
+        held_entered[...], held_multiplied[...], held_turned[...] = flight
         return carry
 
-    lax.fori_loop(0, BLOCKS // batch, body, 0)
+    lax.fori_loop(0, 4, pair_step, 0)
+    flight = held_entered[...], held_multiplied[...], held_turned[...]
+    for step in range(3):
+        ago, last_bin = left_at(step)
+        q = 8 - ago
+        target = (even_back, odd_back)[q % 2]
+        flight = advance(flight, None, 0, target, last_bin)
+        if last_bin + SIZE == 8:
+            for tile in range(TILES):
+                back_low(q, tile, target)
 
     def gather_step(tile, carry):
-        rows = tile_rows(tile)
         scale = 1.0 / LENGTH
-        for q in range(8):
+        for b in range(8):
             column = []
-            for p in range(8):
-                at = q + 8 * p
-                r, i = back[at, rows, :LANES], back[at, rows, LANES:]
-                c, s = load_pair(phases, at)
-                column.append(lift((r * c - i * s, i * c + r * s), tile, at, 1))
-            for b, value in enumerate(dft8(column, 1)):
-                store_pair(first, turn(value, b * (q + 0.25) / 64.0), 8 * b + q)
-        for b in range(8):
-            column = [load_pair(first, 8 * b + q) for q in range(8)]
+            for q in range(8):
+                at = 8 * b + q
+                value = (gathered[tile, at, :, :LANES], gathered[tile, at, :, LANES:])
+                column.append(turn(value, b * (q + 0.25) / 64.0))
             for a, (r, i) in enumerate(dft8(column, 1)):
                 c, s = unit(a / 32.0)
                 results[tile, 8 * a + b] = r * (c * scale) - i * (s * scale)
@@ -301,14 +371,10 @@
 
 
 def outer_phases():
-    position = np.arange(TILE * LANES).reshape(1, TILE, LANES)
-    return side_by_side(position * (np.arange(BLOCKS).reshape(BLOCKS, 1, 1) + 0.25) / LENGTH)
-
-
-def tile_phases():
-    start = TILE * LANES * np.arange(TILES).reshape(TILES, 1, 1)
-    turns = start * (np.arange(BLOCKS).reshape(1, BLOCKS, 1) + 0.25) / LENGTH
-    return side_by_side(np.broadcast_to(turns, (TILES, BLOCKS, LANES)))
+    position = np.arange(ROWS * LANES).reshape(1, ROWS, LANES)
+    bins = np.arange(BLOCKS).reshape(8, 8).T.reshape(BLOCKS, 1, 1)
+    turns = side_by_side(position * (bins + 0.25) / LENGTH)
+    return turns.reshape(8, 8, ROWS, 2 * LANES)
 
 
 def inner_phases():
@@ -321,20 +387,19 @@
     return high, low
 
 
-def rotation(size, inverse):
+def rotation(size):
     angle = 2.0 * np.pi * (np.outer(np.arange(size), np.arange(size)) % size) / size
     c, s = np.cos(angle), np.sin(angle)
-    whole = np.block([[c, s], [-s, c]])
-    return whole.T if inverse else whole
-
-
-def left_table(inverse):
-    high, low = halves(rotation(ROWS, inverse))
-    return np.concatenate([high, low, high], axis=1)
-
-
-def right_table(inverse):
-    high, low = halves(rotation(LANES, inverse).T)
+    return np.block([[c, s], [-s, c]])
+
+
+def left_table():
+    high, low = halves(rotation(ROWS))
+    return np.block([[high, high], [low, np.zeros_like(low)]])
+
+
+def right_table():
+    high, low = halves(rotation(LANES).T)
     return np.concatenate([high, high, low], axis=0)
 
 
@@ -385,12 +450,9 @@
 def correlate(core, arrived, swapped):
     tables = [
         outer_phases(),
-        tile_phases(),
-        left_table(False),
-        left_table(True),
+        left_table(),
         inner_phases(),
-        right_table(False),
-        right_table(True),
+        right_table(),
     ]
     tile = (TILES, BLOCKS, TILE, LANES)
     return pl.pallas_call(
@@ -402,13 +464,20 @@
         + [
             pltpu.VMEM(tile, jnp.float32),
             pltpu.VMEM(tile, jnp.float32),
-            pltpu.VMEM((BLOCKS, TILE, 2 * LANES), jnp.float32),
-            pltpu.VMEM((BLOCKS, 2, ROWS, 2 * LANES), jnp.float32),
-            pltpu.VMEM((BLOCKS, ROWS, 2 * LANES), jnp.float32),
+            pltpu.VMEM((2, TILES, BLOCKS, TILE, 2 * LANES), jnp.float32),
+            pltpu.VMEM((8, 2, ROWS, 2 * LANES), jnp.float32),
+            pltpu.VMEM((8, 2, ROWS, 2 * LANES), jnp.float32),
+            pltpu.VMEM((8, ROWS, 2 * LANES), jnp.float32),
+            pltpu.VMEM((8, ROWS, 2 * LANES), jnp.float32),
+            pltpu.VMEM((TILES, BLOCKS, TILE, 2 * LANES), jnp.float32),
             pltpu.VMEM(tile, jnp.float32),
+            pltpu.VMEM((2 * SIZE * ROWS, 2 * LANES), jnp.float32),
+            pltpu.VMEM((SIZE * ROWS, 2 * LANES), jnp.float32),
+            pltpu.VMEM((2 * ROWS, SIZE * LANES), jnp.float32),
             pltpu.SemaphoreType.DMA((TILES,)),
             pltpu.SemaphoreType.DMA((TILES,)),
             pltpu.SemaphoreType.DMA((len(tables),)),
+            pltpu.SemaphoreType.DMA((8,)),
             pltpu.SemaphoreType.DMA((TILES,)),
         ],
         compiler_params=PARAMS,

time: 126 us -> 120 us (0.952)
  Pallas kernels: 29.7 us -> 23.8 us
    pallas_call x1, Pallas kernels: 24.4 us -> 18.5 us  [correlate(): pl.pallas_call(correlate_kernel, in_specs=[pl.BlockSpec(memory_space=pltp...]
where the time goes in v3:
time: 120 us
  blocking collectives  91.2 us (76%)
  Pallas kernels  23.8 us (20%)
  waiting for transfers between devices  2.63 us (2%)
    all_to_all x2, blocking collectives, exchange(): lax.all_to_all(blocks, ('seqo', 'seqi'), split_axis=0, concat_axis=0, til...  91.2 us
    pallas_call x1, Pallas kernels, correlate(): pl.pallas_call(correlate_kernel, in_specs=[pl.BlockSpec(memory_space=pltp...  18.5 us
    pallas_call x1, Pallas kernels, pack(): pl.pallas_call(pack_kernel, in_specs=[ANY] * 3, out_specs=ANY, out_shape=...  3.01 us
    ppermute x1, waiting for transfers between devices, on_device(): lax.ppermute(arrived[:, ROWS:], 'seqi', [(n, n ^ 1) for n in range(inner)])  2.63 us
  transfers between devices with their start and end apart: 1, of which 1 were waited for; matrix products, arithmetic and copies ran while one was open for 0% of the time, Pallas kernels for 0%

profile of v3, /device:TPU:1, one launch (start us, length us, event | category | flops | bytes accessed | tf_op | source)
XLA Modules:
  0.0 120.0 jit_solution(2507991042868998799)
XLA Ops:
  0.6 3.0 %pack.1 = f32[32,2,96,128]{3,2,1,0:T(8,128)} custom-call(f32[24,8192]{1,0:T(8,128)} %signal.1, f32[24,8192]{1,0:T(8,128)} %cotangent.1, f32[24,8192]{1,0:T(8,128)} %long_filter.1), custom_call_target="tpu_custom_call" | custom-call | tf_op jit(solution)/shard_map/pack/pallas_call | solution.py:415
  3.6 54.8 %all_to_all.10.arrived = f32[64,96,128]{2,1,0:T(8,128)S(1)} all-to-all(f32[64,96,128]{2,1,0:T(8,128)} %bitcast.3), channel_id=1, replica_groups=mesh['seqo'=4,'seqi'=16,'chan'=2] {'seqo','seqi'}, dimensions={0} | all-to-all | bytes 6291456 | tf_op jit(solution)/shard_map/all_to_all | solution.py:489
  58.4 0.0 copy-start
  58.4 1.1 slice.4
  59.5 0.6 collective-permute-start
  60.1 2.6 %collective-permute-done.swapped = f32[64,32,128]{2,1,0:T(8,128)} collective-permute-done((f32[64,32,128]{2,1,0:T(8,128)}, f32[64,32,128]{2,1,0:T(8,128)}, u32[]{:S(2)}, u32[]{:S(2)}) %collective-permute-start) | collective-permute-done | bytes 1048608 | tf_op jit(solution)/shard_map/ppermute | solution.py:498
  62.7 0.0 copy-done
  62.7 18.5 %correlate.1 = f32[64,64,128]{2,1,0:T(8,128)} custom-call(s32[1]{0:T(128)} %bitcast.core, f32[64,96,128]{2,1,0:T(8,128)} %copy-done, f32[64,32,128]{2,1,0:T(8,128)} %collective-permute-done.swapped, f32[8,8,64,256]{3,2,1,0:T(8,128)} %constant.27.clone.refs_0_, bf16[256,256]{1,0:T(8,128)(2,1)} %constant.28.clone.refs_1_, f32[64,256]{1,0:T(8,128)} %constant.29.clone.refs_2_, ...), custom_call_target="tpu_custom_call" | custom-call | tf_op jit(solution)/shard_map/correlate/pallas_call | solution.py:458
  81.3 36.5 %all_to_all.11 = f32[64,64,128]{2,1,0:T(8,128)} all-to-all(f32[64,64,128]{2,1,0:T(8,128)} %correlate.1), channel_id=1, replica_groups=mesh['seqo'=4,'seqi'=16,'chan'=2] {'seqo','seqi'}, dimensions={0} | all-to-all | bytes 4194304 | tf_op jit(solution)/shard_map/all_to_all | solution.py:489
  117.7 2.3 %unpack.1 = (f32[24,8192]{1,0:T(8,128)}, f32[24,8192]{1,0:T(8,128)}) custom-call(f32[32,2,64,128]{3,2,1,0:T(8,128)} %bitcast.4), custom_call_target="tpu_custom_call" | custom-call | tf_op jit(solution)/shard_map/unpack/pallas_call | solution.py:434
Async XLA Ops:
  58.4 4.3 %copy-start = (f32[64,96,128]{2,1,0:T(8,128)}, f32[64,96,128]{2,1,0:T(8,128)S(1)}, u32[]{:S(2)}) copy-start(f32[64,96,128]{2,1,0:T(8,128)S(1)} %all_to_all.10.arrived) | copy-start | bytes 9437188
  59.5 3.2 %collective-permute-start = (f32[64,32,128]{2,1,0:T(8,128)}, f32[64,32,128]{2,1,0:T(8,128)}, u32[]{:S(2)}, u32[]{:S(2)}) collective-permute-start(f32[64,32,128]{2,1,0:T(8,128)} %slice.4), channel_id=1, source_target_pairs={{0,2},{2,0},{4,6},{6,4},{8,10},{10,8},{12,14},{14,12},{16,18},{18,... | collective-permute-start | bytes 3145736 | tf_op jit(solution)/shard_map/ppermute | solution.py:498

commit v4 on v3

--- a/solution.py
+++ b/solution.py
@@ -7,7 +7,7 @@
 from jax import lax
 from jax.experimental import pallas as pl
 from jax.experimental.pallas import tpu as pltpu
-from jax.sharding import PartitionSpec as P
+from jax.sharding import Mesh, PartitionSpec as P
 
 LANES = 128
 BLOCKS = 64
@@ -18,7 +18,14 @@
 SIZE = 4
 STEPS = 8 // SIZE
 LENGTH = BLOCKS * ROWS * LANES
+SEQUENCE = ("z", "y", "xh", "core")
+LISTED = ("core", "z", "xh", "y")
 ROOT_HALF = math.sqrt(0.5)
+
+
+def slot_of(block):
+    z, y, xh, core = block // 16, block // 4 % 4, block // 2 % 2, block % 2
+    return 32 * core + 8 * z + 4 * xh + y
 
 
 def unit(turns):
@@ -87,14 +94,23 @@
 
 def pack_kernel(signal, cotangent, long_filter, out, taken, packed, in_sems, out_sems):
     groups = signal.shape[0] // TILE
+    slots = out.shape[1] // TILE
     sources = (long_filter, signal, cotangent)
 
     def arrival(g, n):
         rows = pl.ds(TILE * g, TILE)
         return pltpu.make_async_copy(sources[n].at[rows], taken.at[g, n], in_sems.at[g, n])
 
-    def departure(g, slot):
-        return pltpu.make_async_copy(packed.at[g], out.at[pl.ds(TILE * slot, TILE)], out_sems.at[slot])
+    def departure(slot, n):
+        g = min(slot, groups - 1)
+        chips = pl.ds(TILE * slot, TILE)
+        if n < 2:
+            rows = pl.ds(0, ROWS)
+            source, target = packed.at[g, n, :, rows], out.at[n, chips, rows]
+        else:
+            rows = pl.ds(ROWS, ROWS // 2)
+            source, target = packed.at[g, :, :, rows], out.at[:, chips, rows]
+        return pltpu.make_async_copy(source, target, out_sems.at[slot, n])
 
     for g in range(groups):
         for n in range(3):
@@ -102,43 +118,46 @@
     for g in range(groups):
         for n in range(3):
             arrival(g, n).wait()
-        for u in range(TILES):
-            for n in range(3):
+            for u in range(TILES):
                 slabs = [
                     taken[g, n, :, (TILE * u + v) * LANES : (TILE * u + v + 1) * LANES]
                     for v in range(TILE)
                 ]
                 turned = jnp.swapaxes(jnp.stack(slabs), 0, 1)
                 if n < 2:
-                    packed[g, :, n, TILE * u : TILE * (u + 1)] = turned
+                    packed[g, n, :, TILE * u : TILE * (u + 1)] = turned
                 else:
                     low = ROWS + TILE * (u % HALF_TILES)
-                    packed[g, :, u // HALF_TILES, low : low + TILE] = turned
-        departure(g, g).start()
-    for slot in range(groups, out.shape[0] // TILE):
-        departure(groups - 1, slot).start()
-    for slot in range(out.shape[0] // TILE):
-        departure(min(slot, groups - 1), slot).wait()
+                    packed[g, u // HALF_TILES, :, low : low + TILE] = turned
+            departure(g, n).start()
+    for slot in range(groups, slots):
+        for n in range(3):
+            departure(slot, n).start()
+    for slot in range(slots):
+        for n in range(3):
+            departure(slot, n).wait()
 
 
 def unpack_kernel(landed, grad_signal, grad_filter, taken, turned_out, in_sems, out_sems):
     groups = grad_signal.shape[0] // TILE
     targets = (grad_signal, grad_filter)
 
-    def arrival(g):
-        return pltpu.make_async_copy(landed.at[pl.ds(TILE * g, TILE)], taken.at[g], in_sems.at[g])
+    def arrival(g, n):
+        chips = pl.ds(TILE * g, TILE)
+        return pltpu.make_async_copy(landed.at[n, chips], taken.at[g, n], in_sems.at[g, n])
 
     def departure(g, n):
         rows = pl.ds(TILE * g, TILE)
         return pltpu.make_async_copy(turned_out.at[g, n], targets[n].at[rows], out_sems.at[g, n])
 
     for g in range(groups):
-        arrival(g).start()
+        for n in range(2):
+            arrival(g, n).start()
     for g in range(groups):
-        arrival(g).wait()
         for n in range(2):
+            arrival(g, n).wait()
             for u in range(TILES):
-                turned = jnp.swapaxes(taken[g, :, n, TILE * u : TILE * (u + 1)], 0, 1)
+                turned = jnp.swapaxes(taken[g, n, :, TILE * u : TILE * (u + 1)], 0, 1)
                 for v in range(TILE):
                     at = (TILE * u + v) * LANES
                     turned_out[g, n, :, at : at + LANES] = turned[v]
@@ -185,7 +204,7 @@
         other_copy(i).start()
     for n in range(1, len(tables)):
         table_copy(n).start()
-    for q in range(8):
+    for q in range(3):
         phase_copy(q).start()
     for ref in (held_entered, held_multiplied, held_turned, even_back, odd_back):
         ref[...] = jnp.zeros(ref.shape, ref.dtype)
@@ -195,7 +214,7 @@
             column = []
             for a in range(8):
                 c, s = unit(-a / 32.0)
-                x = source[slot, 8 * a + b]
+                x = source[slot, slot_of(8 * a + b)]
                 column.append((x * c, x * s))
             for q, value in enumerate(dft8(column, -1)):
                 r, i = turn(value, -b * (q + 0.25) / 64.0)
@@ -213,6 +232,8 @@
     lax.fori_loop(0, TILES, spread_step, 0)
     for n in range(1, len(tables)):
         table_copy(n).wait()
+    for q in range(3, 8):
+        phase_copy(q).start()
     phase_copy(0).wait()
 
     def over_low(q, tile, number, target):
@@ -310,8 +331,9 @@
             ago, last_bin = left_at(step)
             flight = advance(flight, now, step * SIZE, backs[ago % 2], last_bin)
             for n in range(step * per_step, (step + 1) * per_step):
-                over_low(q_next, n // 2, n % 2, then)
-            if last_bin + SIZE == 8:
+                if q_next is not None:
+                    over_low(q_next, n // 2, n % 2, then)
+            if last_bin + SIZE == 8 and q_last is not None:
                 for tile in range(TILES):
                     back_low(q_last, tile, backs[ago % 2])
         return flight
@@ -320,23 +342,30 @@
         over_low(0, tile, 0, even)
         over_low(0, tile, 1, even)
 
+    backs_of = ((even_back, odd_back), (odd_back, even_back))
+    enter_of = ((even, odd), (odd, even))
+    flight = held_entered[...], held_multiplied[...], held_turned[...]
+    for q in range(2):
+        phase_copy(q + 1).wait()
+        flight = half(flight, enter_of[q][0], q + 1, enter_of[q][1], None, backs_of[q])
+    held_entered[...], held_multiplied[...], held_turned[...] = flight
+
     def pair_step(t, carry):
-        phase_copy(2 * t + 1).wait()
-
-        @pl.when(t < 3)
-        def _():
-            phase_copy(2 * t + 2).wait()
-
         flight = held_entered[...], held_multiplied[...], held_turned[...]
-        last = jnp.maximum(2 * t - delay, 0)
-        flight = half(flight, even, 2 * t + 1, odd, last, (even_back, odd_back))
-        last = jnp.maximum(2 * t + 1 - delay, 0)
-        flight = half(flight, odd, jnp.minimum(2 * t + 2, 7), even, last, (odd_back, even_back))
+        for n in range(2):
+            phase_copy(2 * t + n + 1).wait()
+        for n in range(2):
+            q = 2 * t + n
+            flight = half(flight, enter_of[n][0], q + 1, enter_of[n][1], q - delay, backs_of[n])
         held_entered[...], held_multiplied[...], held_turned[...] = flight
         return carry
 
-    lax.fori_loop(0, 4, pair_step, 0)
+    lax.fori_loop(1, 3, pair_step, 0, unroll=2)
+    phase_copy(7).wait()
     flight = held_entered[...], held_multiplied[...], held_turned[...]
+    for q in range(6, 8):
+        after = q + 1 if q < 7 else None
+        flight = half(flight, enter_of[q % 2][0], after, enter_of[q % 2][1], q - delay, backs_of[q % 2])
     for step in range(3):
         ago, last_bin = left_at(step)
         q = 8 - ago
@@ -356,7 +385,7 @@
                 column.append(turn(value, b * (q + 0.25) / 64.0))
             for a, (r, i) in enumerate(dft8(column, 1)):
                 c, s = unit(a / 32.0)
-                results[tile, 8 * a + b] = r * (c * scale) - i * (s * scale)
+                results[tile, slot_of(8 * a + b)] = r * (c * scale) - i * (s * scale)
         out_copy(tile).start()
         return carry
 
@@ -416,12 +445,12 @@
         pack_kernel,
         in_specs=[ANY] * 3,
         out_specs=ANY,
-        out_shape=jax.ShapeDtypeStruct((chips, 2, height, LANES), jnp.float32),
+        out_shape=jax.ShapeDtypeStruct((2, chips, height, LANES), jnp.float32),
         scratch_shapes=[
             pltpu.VMEM((groups, 3, TILE, ROWS * LANES), jnp.float32),
-            pltpu.VMEM((groups, TILE, 2, height, LANES), jnp.float32),
+            pltpu.VMEM((groups, 2, TILE, height, LANES), jnp.float32),
             pltpu.SemaphoreType.DMA((groups, 3)),
-            pltpu.SemaphoreType.DMA((chips // TILE,)),
+            pltpu.SemaphoreType.DMA((chips // TILE, 3)),
         ],
         compiler_params=PARAMS,
         name="pack",
@@ -437,9 +466,9 @@
         out_specs=[ANY, ANY],
         out_shape=[result, result],
         scratch_shapes=[
-            pltpu.VMEM((groups, TILE, 2, ROWS, LANES), jnp.float32),
+            pltpu.VMEM((groups, 2, TILE, ROWS, LANES), jnp.float32),
             pltpu.VMEM((groups, 2, TILE, ROWS * LANES), jnp.float32),
-            pltpu.SemaphoreType.DMA((groups,)),
+            pltpu.SemaphoreType.DMA((groups, 2)),
             pltpu.SemaphoreType.DMA((groups, 2)),
         ],
         compiler_params=PARAMS,
@@ -486,23 +515,22 @@
 
 
 def exchange(blocks):
-    return lax.all_to_all(blocks, ("seqo", "seqi"), split_axis=0, concat_axis=0, tiled=True)
+    return lax.all_to_all(blocks, LISTED, split_axis=0, concat_axis=0, tiled=True)
 
 
 def on_device(signal, cotangent, long_filter):
     channels = signal.shape[0]
-    inner = lax.axis_size("seqi")
-    members = lax.axis_size("seqo") * inner
-    packed = pack(signal, cotangent, long_filter, members // 2)
-    arrived = exchange(packed.reshape(members, *packed.shape[2:]))
-    swapped = lax.ppermute(arrived[:, ROWS:], "seqi", [(n, n ^ 1) for n in range(inner)])
-    core = (lax.axis_index("seqi") % 2).astype(jnp.int32).reshape(1)
+    packed = pack(signal, cotangent, long_filter, BLOCKS // 2)
+    arrived = exchange(packed.reshape(BLOCKS, *packed.shape[2:]))
+    swapped = lax.ppermute(arrived[:, ROWS:], "core", [(0, 1), (1, 0)])
+    core = lax.axis_index("core").astype(jnp.int32).reshape(1)
     landed = exchange(correlate(core, arrived, swapped))
-    return tuple(unpack(landed.reshape(members // 2, 2, ROWS, LANES), channels))
+    return tuple(unpack(landed.reshape(2, BLOCKS // 2, ROWS, LANES), channels))
 
 
 def solution(mesh):
-    spec = P("chan", ("seqo", "seqi"))
+    digits = Mesh(mesh.devices.reshape(4, 4, 2, 2, 2), SEQUENCE + ("chan",))
+    spec = P("chan", SEQUENCE)
     return jax.shard_map(
-        on_device, mesh=mesh, in_specs=(spec,) * 3, out_specs=(spec,) * 2, check_vma=False
+        on_device, mesh=digits, in_specs=(spec,) * 3, out_specs=(spec,) * 2, check_vma=False
     )

time: 120 us -> 117 us (0.975)
  blocking collectives: 91.2 us -> 87.8 us
    all_to_all x2, blocking collectives: 91.2 us -> 87.8 us  [exchange(): lax.all_to_all(blocks, LISTED, split_axis=0, concat_axis=0, tiled=True)]
where the time goes in v4:
time: 117 us; the launch traced here: 116 us
  blocking collectives  87.8 us (75%)
  Pallas kernels  23.3 us (20%)
  waiting for transfers between devices  2.63 us (2%)
    all_to_all x2, blocking collectives, exchange(): lax.all_to_all(blocks, LISTED, split_axis=0, concat_axis=0, tiled=True)  87.8 us
    pallas_call x1, Pallas kernels, correlate(): pl.pallas_call(correlate_kernel, in_specs=[pl.BlockSpec(memory_space=pltp...  18.1 us
    pallas_call x1, Pallas kernels, pack(): pl.pallas_call(pack_kernel, in_specs=[ANY] * 3, out_specs=ANY, out_shape=...  2.9 us
    ppermute x1, waiting for transfers between devices, on_device(): swapped = lax.ppermute(arrived[:, ROWS:], 'core', [(0, 1), (1, 0)])  2.63 us
  transfers between devices with their start and end apart: 1, of which 1 were waited for; matrix products, arithmetic and copies ran while one was open for 0% of the time, Pallas kernels for 0%

profile of v4, /device:TPU:1, one launch (start us, length us, event | category | flops | bytes accessed | tf_op | source)
XLA Modules:
  0.0 116.5 jit_solution(15152763038518121897)
XLA Ops:
  0.6 2.9 %pack.1 = f32[2,32,96,128]{3,2,1,0:T(8,128)} custom-call(f32[24,8192]{1,0:T(8,128)} %signal.1, f32[24,8192]{1,0:T(8,128)} %cotangent.1, f32[24,8192]{1,0:T(8,128)} %long_filter.1), custom_call_target="tpu_custom_call" | custom-call | tf_op jit(solution)/shard_map/pack/pallas_call | solution.py:444
  3.5 53.2 %all_to_all.10.arrived = f32[64,96,128]{2,1,0:T(8,128)S(1)} all-to-all(f32[64,96,128]{2,1,0:T(8,128)} %bitcast.3), channel_id=1, replica_groups=mesh['z'=4,'y'=4,'xh'=2,'core'=2,'chan'=2] {'core','z','xh','y'}, dimensions={0} | all-to-all | bytes 6291456 | tf_op jit(solution)/shard_map/all_to_all | solution.py:518
  56.7 0.0 copy-start
  56.8 1.1 slice.4
  57.9 0.9 collective-permute-start
  58.7 2.6 %collective-permute-done.swapped = f32[64,32,128]{2,1,0:T(8,128)} collective-permute-done((f32[64,32,128]{2,1,0:T(8,128)}, f32[64,32,128]{2,1,0:T(8,128)}, u32[]{:S(2)}, u32[]{:S(2)}) %collective-permute-start) | collective-permute-done | bytes 1048608 | tf_op jit(solution)/shard_map/ppermute | solution.py:525
  61.4 0.0 copy-done
  61.4 18.1 %correlate.1 = f32[64,64,128]{2,1,0:T(8,128)} custom-call(s32[1]{0:T(128)} %bitcast.core, f32[64,96,128]{2,1,0:T(8,128)} %copy-done, f32[64,32,128]{2,1,0:T(8,128)} %collective-permute-done.swapped, f32[8,8,64,256]{3,2,1,0:T(8,128)} %constant.12.clone.refs_0_, bf16[256,256]{1,0:T(8,128)(2,1)} %constant.13.clone.refs_1_, f32[64,256]{1,0:T(8,128)} %constant.14.clone.refs_2_, ...), custom_call_target="tpu_custom_call" | custom-call | tf_op jit(solution)/shard_map/correlate/pallas_call | solution.py:487
  79.5 34.6 %all_to_all.11 = f32[64,64,128]{2,1,0:T(8,128)} all-to-all(f32[64,64,128]{2,1,0:T(8,128)} %correlate.1), channel_id=1, replica_groups=mesh['z'=4,'y'=4,'xh'=2,'core'=2,'chan'=2] {'core','z','xh','y'}, dimensions={0} | all-to-all | bytes 4194304 | tf_op jit(solution)/shard_map/all_to_all | solution.py:518
  114.1 2.2 %unpack.1 = (f32[24,8192]{1,0:T(8,128)}, f32[24,8192]{1,0:T(8,128)}) custom-call(f32[2,32,64,128]{3,2,1,0:T(8,128)} %bitcast.4), custom_call_target="tpu_custom_call" | custom-call | tf_op jit(solution)/shard_map/unpack/pallas_call | solution.py:463
Async XLA Ops:
  56.7 4.6 %copy-start = (f32[64,96,128]{2,1,0:T(8,128)}, f32[64,96,128]{2,1,0:T(8,128)S(1)}, u32[]{:S(2)}) copy-start(f32[64,96,128]{2,1,0:T(8,128)S(1)} %all_to_all.10.arrived) | copy-start | bytes 9437188
  57.9 3.5 %collective-permute-start = (f32[64,32,128]{2,1,0:T(8,128)}, f32[64,32,128]{2,1,0:T(8,128)}, u32[]{:S(2)}, u32[]{:S(2)}) collective-permute-start(f32[64,32,128]{2,1,0:T(8,128)} %slice.4), channel_id=1, source_target_pairs={{0,2},{2,0},{1,3},{3,1},{4,6},{6,4},{5,7},{7,5},{8,10},{10,8},{9,1... | collective-permute-start | bytes 3145736 | tf_op jit(solution)/shard_map/ppermute | solution.py:525

commit v5 on v4

--- a/solution.py
+++ b/solution.py
@@ -432,7 +432,8 @@
     return np.concatenate([high, high, low], axis=0)
 
 
-PARAMS = pltpu.CompilerParams(vmem_limit_bytes=56 * 1024 * 1024)
+MIB = 1024 * 1024
+PARAMS = pltpu.CompilerParams(vmem_limit_bytes=56 * MIB)
 
 
 ANY = pl.BlockSpec(memory_space=pl.ANY)
@@ -471,7 +472,7 @@
             pltpu.SemaphoreType.DMA((groups, 2)),
             pltpu.SemaphoreType.DMA((groups, 2)),
         ],
-        compiler_params=PARAMS,
+        compiler_params=pltpu.CompilerParams(vmem_limit_bytes=16 * MIB),
         name="unpack",
     )(landed)
 
@@ -509,7 +510,7 @@
             pltpu.SemaphoreType.DMA((8,)),
             pltpu.SemaphoreType.DMA((TILES,)),
         ],
-        compiler_params=PARAMS,
+        compiler_params=pltpu.CompilerParams(vmem_limit_bytes=40 * MIB),
         name="correlate",
     )(core, arrived, swapped, *tables)
 

time: 117 us -> 119 us (1.017)
  local copies, waits for them, and re-layouts: 1.11 us -> 4.97 us
    unnamed x2 -> x8, local copies, waits for them, and re-layouts: 0.01 us -> 3.94 us
where the time goes in v5:
time: 119 us
  blocking collectives  87.5 us (74%)
  Pallas kernels  22.3 us (19%)
  local copies, waits for them, and re-layouts  4.97 us (4%)
  waiting for transfers between devices  2.63 us (2%)
    all_to_all x2, blocking collectives, exchange(): lax.all_to_all(blocks, LISTED, split_axis=0, concat_axis=0, tiled=True)  87.5 us
    pallas_call x1, Pallas kernels, correlate(): pl.pallas_call(correlate_kernel, in_specs=[pl.BlockSpec(memory_space=pltp...  18.1 us
    unnamed x8, local copies, waits for them, and re-layouts  3.94 us
    pallas_call x1, Pallas kernels, pack(): pl.pallas_call(pack_kernel, in_specs=[ANY] * 3, out_specs=ANY, out_shape=...  2.86 us
    ppermute x1, waiting for transfers between devices, on_device(): swapped = lax.ppermute(arrived[:, ROWS:], 'core', [(0, 1), (1, 0)])  2.63 us
  transfers between devices with their start and end apart: 1, of which 1 were waited for; matrix products, arithmetic and copies ran while one was open for 0% of the time, Pallas kernels for 0%

profile of v5, /device:TPU:1, one launch (start us, length us, event | category | flops | bytes accessed | tf_op | source)
XLA Modules:
  0.0 119.1 jit_solution(6033782005696935525)
XLA Ops:
  0.6 2.9 %pack.1 = f32[2,32,96,128]{3,2,1,0:T(8,128)} custom-call(f32[24,8192]{1,0:T(8,128)} %signal.1, f32[24,8192]{1,0:T(8,128)} %cotangent.1, f32[24,8192]{1,0:T(8,128)} %long_filter.1), custom_call_target="tpu_custom_call" | custom-call | tf_op jit(solution)/shard_map/pack/pallas_call | solution.py:445
  3.5 0.0 copy-start.1
  3.5 53.3 %all_to_all.10.arrived = f32[64,96,128]{2,1,0:T(8,128)S(1)} all-to-all(f32[64,96,128]{2,1,0:T(8,128)} %bitcast.4), channel_id=1, replica_groups=mesh['z'=4,'y'=4,'xh'=2,'core'=2,'chan'=2] {'core','z','xh','y'}, dimensions={0} | all-to-all | bytes 6291456 | tf_op jit(solution)/shard_map/all_to_all | solution.py:519
  56.9 1.0 slice.4
  57.9 0.9 collective-permute-start
  58.8 2.6 %collective-permute-done.swapped = f32[64,32,128]{2,1,0:T(8,128)} collective-permute-done((f32[64,32,128]{2,1,0:T(8,128)}, f32[64,32,128]{2,1,0:T(8,128)}, u32[]{:S(2)}, u32[]{:S(2)}) %collective-permute-start) | collective-permute-done | bytes 1048608 | tf_op jit(solution)/shard_map/ppermute | solution.py:526
  61.4 0.0 copy-done.1
  61.4 0.0 copy-start
  61.4 2.2 %copy-done = f32[8,8,64,256]{3,2,1,0:T(8,128)S(1)} copy-done((f32[8,8,64,256]{3,2,1,0:T(8,128)S(1)}, f32[8,8,64,256]{3,2,1,0:T(8,128)}, u32[]{:S(2)}) %copy-start) | copy-done | bytes 4194328
  63.6 0.0 copy-start.2
  63.6 0.9 copy-done.2
  64.5 0.0 copy-start.3
  64.5 0.8 copy-done.3
  65.3 18.1 %correlate.1 = f32[64,64,128]{2,1,0:T(8,128)S(1)} custom-call(s32[1]{0:T(128)} %bitcast.core, f32[64,96,128]{2,1,0:T(8,128)S(1)} %all_to_all.10.arrived, f32[64,32,128]{2,1,0:T(8,128)} %collective-permute-done.swapped, f32[8,8,64,256]{3,2,1,0:T(8,128)S(1)} %copy-done, bf16[256,256]{1,0:T(8,128)(2,1)S(1)} %copy-done.2, f32[64,256]{1,0:T(8,128)S(1)} %copy-done.3, ...), custom_call_target="tpu_custom_call" | custom-call | tf_op jit(solution)/shard_map/correlate/pallas_call | solution.py:488
  83.4 34.2 %all_to_all.11 = f32[64,64,128]{2,1,0:T(8,128)S(1)} all-to-all(f32[64,64,128]{2,1,0:T(8,128)S(1)} %correlate.1), channel_id=1, replica_groups=mesh['z'=4,'y'=4,'xh'=2,'core'=2,'chan'=2] {'core','z','xh','y'}, dimensions={0} | all-to-all | bytes 4194304 | tf_op jit(solution)/shard_map/all_to_all | solution.py:519
  117.5 1.4 %unpack.1 = (f32[24,8192]{1,0:T(8,128)}, f32[24,8192]{1,0:T(8,128)}) custom-call(f32[2,32,64,128]{3,2,1,0:T(8,128)S(1)} %bitcast.3), custom_call_target="tpu_custom_call" | custom-call | tf_op jit(solution)/shard_map/unpack/pallas_call | solution.py:464
Async XLA Ops:
  3.5 57.9 %copy-start.1 = (bf16[768,256]{1,0:T(8,128)(2,1)S(1)}, bf16[768,256]{1,0:T(8,128)(2,1)}, u32[]{:S(2)}) copy-start(bf16[768,256]{1,0:T(8,128)(2,1)} %constant.15.clone.refs_3_) | copy-start | bytes 1179652
  57.9 3.5 %collective-permute-start = (f32[64,32,128]{2,1,0:T(8,128)}, f32[64,32,128]{2,1,0:T(8,128)}, u32[]{:S(2)}, u32[]{:S(2)}) collective-permute-start(f32[64,32,128]{2,1,0:T(8,128)} %slice.4), channel_id=1, source_target_pairs={{0,2},{2,0},{1,3},{3,1},{4,6},{6,4},{5,7},{7,5},{8,10},{10,8},{9,1... | collective-permute-start | bytes 3145736 | tf_op jit(solution)/shard_map/ppermute | solution.py:526
  61.4 2.2 %copy-start = (f32[8,8,64,256]{3,2,1,0:T(8,128)S(1)}, f32[8,8,64,256]{3,2,1,0:T(8,128)}, u32[]{:S(2)}) copy-start(f32[8,8,64,256]{3,2,1,0:T(8,128)} %constant.12.clone.refs_0_) | copy-start | bytes 12582916
  63.6 0.9 copy-start.2
  64.5 0.8 copy-start.3

commit v6 on v5

--- a/solution.py
+++ b/solution.py
@@ -510,7 +510,7 @@
             pltpu.SemaphoreType.DMA((8,)),
             pltpu.SemaphoreType.DMA((TILES,)),
         ],
-        compiler_params=pltpu.CompilerParams(vmem_limit_bytes=40 * MIB),
+        compiler_params=PARAMS,
         name="correlate",
     )(core, arrived, swapped, *tables)
 

time: 119 us -> 116 us (0.975)
  local copies, waits for them, and re-layouts: 4.97 us -> 1.11 us
    unnamed x8 -> x2, local copies, waits for them, and re-layouts: 3.94 us -> 0.01 us
where the time goes in v6:
time: 116 us; the launch traced here: 115 us
  blocking collectives  87.6 us (76%)
  Pallas kernels  22.4 us (19%)
  waiting for transfers between devices  2.63 us (2%)
    all_to_all x2, blocking collectives, exchange(): lax.all_to_all(blocks, LISTED, split_axis=0, concat_axis=0, tiled=True)  87.6 us
    pallas_call x1, Pallas kernels, correlate(): pl.pallas_call(correlate_kernel, in_specs=[pl.BlockSpec(memory_space=pltp...  18.1 us
    pallas_call x1, Pallas kernels, pack(): pl.pallas_call(pack_kernel, in_specs=[ANY] * 3, out_specs=ANY, out_shape=...  2.9 us
    ppermute x1, waiting for transfers between devices, on_device(): swapped = lax.ppermute(arrived[:, ROWS:], 'core', [(0, 1), (1, 0)])  2.63 us
  transfers between devices with their start and end apart: 1, of which 1 were waited for; matrix products, arithmetic and copies ran while one was open for 0% of the time, Pallas kernels for 0%

profile of v6, /device:TPU:1, one launch (start us, length us, event | category | flops | bytes accessed | tf_op | source)
XLA Modules:
  0.0 115.4 jit_solution(10927768577293722117)
XLA Ops:
  0.6 2.9 %pack.1 = f32[2,32,96,128]{3,2,1,0:T(8,128)} custom-call(f32[24,8192]{1,0:T(8,128)} %signal.1, f32[24,8192]{1,0:T(8,128)} %cotangent.1, f32[24,8192]{1,0:T(8,128)} %long_filter.1), custom_call_target="tpu_custom_call" | custom-call | tf_op jit(solution)/shard_map/pack/pallas_call | solution.py:445
  3.5 53.2 %all_to_all.10.arrived = f32[64,96,128]{2,1,0:T(8,128)S(1)} all-to-all(f32[64,96,128]{2,1,0:T(8,128)} %bitcast.4), channel_id=1, replica_groups=mesh['z'=4,'y'=4,'xh'=2,'core'=2,'chan'=2] {'core','z','xh','y'}, dimensions={0} | all-to-all | bytes 6291456 | tf_op jit(solution)/shard_map/all_to_all | solution.py:519
  56.7 0.0 copy-start
  56.8 1.1 slice.4
  57.9 0.9 collective-permute-start
  58.7 2.6 %collective-permute-done.swapped = f32[64,32,128]{2,1,0:T(8,128)} collective-permute-done((f32[64,32,128]{2,1,0:T(8,128)}, f32[64,32,128]{2,1,0:T(8,128)}, u32[]{:S(2)}, u32[]{:S(2)}) %collective-permute-start) | collective-permute-done | bytes 1048608 | tf_op jit(solution)/shard_map/ppermute | solution.py:526
  61.4 0.0 copy-done
  61.4 18.1 %correlate.1 = f32[64,64,128]{2,1,0:T(8,128)} custom-call(s32[1]{0:T(128)} %bitcast.core, f32[64,96,128]{2,1,0:T(8,128)} %copy-done, f32[64,32,128]{2,1,0:T(8,128)} %collective-permute-done.swapped, f32[8,8,64,256]{3,2,1,0:T(8,128)} %constant.12.clone.refs_0_, bf16[256,256]{1,0:T(8,128)(2,1)} %constant.13.clone.refs_1_, f32[64,256]{1,0:T(8,128)} %constant.14.clone.refs_2_, ...), custom_call_target="tpu_custom_call" | custom-call | tf_op jit(solution)/shard_map/correlate/pallas_call | solution.py:488
  79.5 34.4 %all_to_all.11 = f32[64,64,128]{2,1,0:T(8,128)S(1)} all-to-all(f32[64,64,128]{2,1,0:T(8,128)} %correlate.1), channel_id=1, replica_groups=mesh['z'=4,'y'=4,'xh'=2,'core'=2,'chan'=2] {'core','z','xh','y'}, dimensions={0} | all-to-all | bytes 4194304 | tf_op jit(solution)/shard_map/all_to_all | solution.py:519
  113.9 1.4 %unpack.1 = (f32[24,8192]{1,0:T(8,128)}, f32[24,8192]{1,0:T(8,128)}) custom-call(f32[2,32,64,128]{3,2,1,0:T(8,128)S(1)} %bitcast.3), custom_call_target="tpu_custom_call" | custom-call | tf_op jit(solution)/shard_map/unpack/pallas_call | solution.py:464
Async XLA Ops:
  56.7 4.6 %copy-start = (f32[64,96,128]{2,1,0:T(8,128)}, f32[64,96,128]{2,1,0:T(8,128)S(1)}, u32[]{:S(2)}) copy-start(f32[64,96,128]{2,1,0:T(8,128)S(1)} %all_to_all.10.arrived) | copy-start | bytes 9437188
  57.9 3.5 %collective-permute-start = (f32[64,32,128]{2,1,0:T(8,128)}, f32[64,32,128]{2,1,0:T(8,128)}, u32[]{:S(2)}, u32[]{:S(2)}) collective-permute-start(f32[64,32,128]{2,1,0:T(8,128)} %slice.4), channel_id=1, source_target_pairs={{0,2},{2,0},{1,3},{3,1},{4,6},{6,4},{5,7},{7,5},{8,10},{10,8},{9,1... | collective-permute-start | bytes 3145736 | tf_op jit(solution)/shard_map/ppermute | solution.py:526

commit v7 on v6

--- a/solution.py
+++ b/solution.py
@@ -94,23 +94,21 @@
 
 def pack_kernel(signal, cotangent, long_filter, out, taken, packed, in_sems, out_sems):
     groups = signal.shape[0] // TILE
-    slots = out.shape[1] // TILE
     sources = (long_filter, signal, cotangent)
 
     def arrival(g, n):
         rows = pl.ds(TILE * g, TILE)
         return pltpu.make_async_copy(sources[n].at[rows], taken.at[g, n], in_sems.at[g, n])
 
-    def departure(slot, n):
-        g = min(slot, groups - 1)
-        chips = pl.ds(TILE * slot, TILE)
+    def departure(g, n):
+        chips = pl.ds(TILE * g, TILE)
         if n < 2:
             rows = pl.ds(0, ROWS)
             source, target = packed.at[g, n, :, rows], out.at[n, chips, rows]
         else:
             rows = pl.ds(ROWS, ROWS // 2)
             source, target = packed.at[g, :, :, rows], out.at[:, chips, rows]
-        return pltpu.make_async_copy(source, target, out_sems.at[slot, n])
+        return pltpu.make_async_copy(source, target, out_sems.at[g, n])
 
     for g in range(groups):
         for n in range(3):
@@ -130,12 +128,9 @@
                     low = ROWS + TILE * (u % HALF_TILES)
                     packed[g, u // HALF_TILES, :, low : low + TILE] = turned
             departure(g, n).start()
-    for slot in range(groups, slots):
+    for g in range(groups):
         for n in range(3):
-            departure(slot, n).start()
-    for slot in range(slots):
-        for n in range(3):
-            departure(slot, n).wait()
+            departure(g, n).wait()
 
 
 def unpack_kernel(landed, grad_signal, grad_filter, taken, turned_out, in_sems, out_sems):
@@ -451,7 +446,7 @@
             pltpu.VMEM((groups, 3, TILE, ROWS * LANES), jnp.float32),
             pltpu.VMEM((groups, 2, TILE, height, LANES), jnp.float32),
             pltpu.SemaphoreType.DMA((groups, 3)),
-            pltpu.SemaphoreType.DMA((chips // TILE, 3)),
+            pltpu.SemaphoreType.DMA((groups, 3)),
         ],
         compiler_params=PARAMS,
         name="pack",

time: 116 us -> 115 us (level)
  no operation moved by 1% of the time
where the time goes in v7:
time: 115 us
  blocking collectives  87.6 us (76%)
  Pallas kernels  22.1 us (19%)
  waiting for transfers between devices  2.63 us (2%)
    all_to_all x2, blocking collectives, exchange(): lax.all_to_all(blocks, LISTED, split_axis=0, concat_axis=0, tiled=True)  87.6 us
    pallas_call x1, Pallas kernels, correlate(): pl.pallas_call(correlate_kernel, in_specs=[pl.BlockSpec(memory_space=pltp...  18.1 us
    ppermute x1, waiting for transfers between devices, on_device(): swapped = lax.ppermute(arrived[:, ROWS:], 'core', [(0, 1), (1, 0)])  2.63 us
    pallas_call x1, Pallas kernels, pack(): pl.pallas_call(pack_kernel, in_specs=[ANY] * 3, out_specs=ANY, out_shape=...  2.58 us
  transfers between devices with their start and end apart: 1, of which 1 were waited for; matrix products, arithmetic and copies ran while one was open for 0% of the time, Pallas kernels for 0%

profile of v7, /device:TPU:1, one launch (start us, length us, event | category | flops | bytes accessed | tf_op | source)
XLA Modules:
  0.0 115.1 jit_solution(11905354306296960161)
XLA Ops:
  0.6 2.6 %pack.1 = f32[2,32,96,128]{3,2,1,0:T(8,128)} custom-call(f32[24,8192]{1,0:T(8,128)} %signal.1, f32[24,8192]{1,0:T(8,128)} %cotangent.1, f32[24,8192]{1,0:T(8,128)} %long_filter.1), custom_call_target="tpu_custom_call" | custom-call | tf_op jit(solution)/shard_map/pack/pallas_call | solution.py:440
  3.2 53.2 %all_to_all.10.arrived = f32[64,96,128]{2,1,0:T(8,128)S(1)} all-to-all(f32[64,96,128]{2,1,0:T(8,128)} %bitcast.4), channel_id=1, replica_groups=mesh['z'=4,'y'=4,'xh'=2,'core'=2,'chan'=2] {'core','z','xh','y'}, dimensions={0} | all-to-all | bytes 6291456 | tf_op jit(solution)/shard_map/all_to_all | solution.py:514
  56.4 0.0 copy-start
  56.4 1.1 slice.4
  57.5 0.9 collective-permute-start
  58.4 2.6 %collective-permute-done.swapped = f32[64,32,128]{2,1,0:T(8,128)} collective-permute-done((f32[64,32,128]{2,1,0:T(8,128)}, f32[64,32,128]{2,1,0:T(8,128)}, u32[]{:S(2)}, u32[]{:S(2)}) %collective-permute-start) | collective-permute-done | bytes 1048608 | tf_op jit(solution)/shard_map/ppermute | solution.py:521
  61.0 0.0 copy-done
  61.0 18.1 %correlate.1 = f32[64,64,128]{2,1,0:T(8,128)} custom-call(s32[1]{0:T(128)} %bitcast.core, f32[64,96,128]{2,1,0:T(8,128)} %copy-done, f32[64,32,128]{2,1,0:T(8,128)} %collective-permute-done.swapped, f32[8,8,64,256]{3,2,1,0:T(8,128)} %constant.12.clone.refs_0_, bf16[256,256]{1,0:T(8,128)(2,1)} %constant.13.clone.refs_1_, f32[64,256]{1,0:T(8,128)} %constant.14.clone.refs_2_, ...), custom_call_target="tpu_custom_call" | custom-call | tf_op jit(solution)/shard_map/correlate/pallas_call | solution.py:483
  79.2 34.4 %all_to_all.11 = f32[64,64,128]{2,1,0:T(8,128)S(1)} all-to-all(f32[64,64,128]{2,1,0:T(8,128)} %correlate.1), channel_id=1, replica_groups=mesh['z'=4,'y'=4,'xh'=2,'core'=2,'chan'=2] {'core','z','xh','y'}, dimensions={0} | all-to-all | bytes 4194304 | tf_op jit(solution)/shard_map/all_to_all | solution.py:514
  113.6 1.4 %unpack.1 = (f32[24,8192]{1,0:T(8,128)}, f32[24,8192]{1,0:T(8,128)}) custom-call(f32[2,32,64,128]{3,2,1,0:T(8,128)S(1)} %bitcast.3), custom_call_target="tpu_custom_call" | custom-call | tf_op jit(solution)/shard_map/unpack/pallas_call | solution.py:459
Async XLA Ops:
  56.4 4.6 %copy-start = (f32[64,96,128]{2,1,0:T(8,128)}, f32[64,96,128]{2,1,0:T(8,128)S(1)}, u32[]{:S(2)}) copy-start(f32[64,96,128]{2,1,0:T(8,128)S(1)} %all_to_all.10.arrived) | copy-start | bytes 9437188
  57.5 3.5 %collective-permute-start = (f32[64,32,128]{2,1,0:T(8,128)}, f32[64,32,128]{2,1,0:T(8,128)}, u32[]{:S(2)}, u32[]{:S(2)}) collective-permute-start(f32[64,32,128]{2,1,0:T(8,128)} %slice.4), channel_id=1, source_target_pairs={{0,2},{2,0},{1,3},{3,1},{4,6},{6,4},{5,7},{7,5},{8,10},{10,8},{9,1... | collective-permute-start | bytes 3145736 | tf_op jit(solution)/shard_map/ppermute | solution.py:521
